TPU v7x, 32 devices: a whole 2x2x4 slice. The times are simulated.
32 devices in a mesh: blk: 16 (over z, y, core), shell: 2 (over x).
Axes of the slice: x: 2, y: 2, z: 4, core: 2. Of those that a mesh axis runs over, the one named last changes fastest.
Arguments:
- images: bfloat16 [8192, 2, 8192], P('blk', None, 'shell'), may hold values from -30 to 30
- references: bfloat16 [1024, 2, 8192], P('blk', None, 'shell'), may hold values from -0.12 to 0.12
- defocus: float32 [8192], P('blk'), may hold values from 20 to 60
- frequency_squared: float32 [8192], P('shell'), may hold values from 0.05 to 1
- shell_index: int32 [8192], P('shell'), may hold values from 0 to 63, never falling along the last dimension, each value on 1 to 256 neighbouring positions
- noise_power: float32 [64], replicated, may hold values from 0.5 to 4
- live_count: int32 [16], P('blk'), may hold values from 1 to 512, 5120 in all
Outputs:
- weighted_images: float32 [1024, 2, 8192], P('blk', None, 'shell')
- weighted_envelope: float32 [1024, 8192], P('blk', 'shell')
- log_evidence: float32 [8192], P('blk')
Inputs may be any that keep to these rules, and one draw needn't show every extreme that they name: `shell_index`: shell numbers never fall along the pixels; a shell holds 1 to 256 pixels. `live_count`: the live particles of a block fill its first slots; some block is full.
All inputs are finite; a program needn't handle non-finite values.
Results may differ from a plain program's by a relative error of at most 0.0059.
Values may be sent and summed in bfloat16 or wider, within the bound.
A program may use at most 128 MiB of HBM per device.

v0:
```python
import jax
import jax.numpy as jnp
from jax import lax
from jax.sharding import PartitionSpec as P

STEPS = 2


def passed_along(value, axis, steps):
    count = lax.axis_size(axis)
    pairs = [(source, (source + steps) % count) for source in range(count)]
    return lax.ppermute(value, axis, pairs)


def body(images, references, defocus, frequency_squared, shell_index, noise_power, live_count):
    capacity = images.shape[0]
    per_block = references.shape[0]
    shells = noise_power.shape[0]
    lookup = jnp.where(
        jnp.arange(shells, dtype=jnp.int32)[:, None] == shell_index[None, :],
        noise_power[:, None],
        0.0,
    )
    weight = 1.0 / jnp.sum(lookup, axis=0)
    contrast = -jnp.sin(defocus[:, None] * frequency_squared[None, :] + 0.1)
    filtered = (images.astype(jnp.float32) * (contrast * weight)[:, None, :]).astype(jnp.bfloat16)
    envelope = (contrast * contrast * (0.5 * weight)).astype(jnp.bfloat16)
    blocks = [references]
    for cycle_step in range(1, STEPS + 1):
        blocks.append(passed_along(blocks[-1], "blk", 1))
    visited = jnp.concatenate(blocks, 0)
    reference_power = (
        jnp.square(visited[:, 0].astype(jnp.float32))
        + jnp.square(visited[:, 1].astype(jnp.float32))
    ).astype(jnp.bfloat16)
    occupied_count = live_count[0]
    crossed = jnp.einsum("rkp,ikp->ri", visited, filtered, preferred_element_type=jnp.float32)
    quadratic = jnp.einsum(
        "rp,ip->ri", reference_power, envelope, preferred_element_type=jnp.float32
    )
    partial_scores = crossed - quadratic
    scores = lax.psum(partial_scores, "shell")
    live_slots = jnp.arange(capacity, dtype=jnp.int32) < occupied_count
    highest = jnp.max(scores, axis=0)
    summed = jnp.sum(jnp.exp(scores - highest[None, :]), axis=0)
    evidence = jnp.where(live_slots, highest + jnp.log(summed), 0.0)
    posterior = jnp.where(live_slots[None, :], jnp.exp(scores - evidence[None, :]), 0.0).astype(
        jnp.bfloat16
    )
    numerator = jnp.einsum("ri,ikp->rkp", posterior, filtered, preferred_element_type=jnp.float32)
    denominator = jnp.einsum("ri,ip->rp", posterior, envelope, preferred_element_type=jnp.float32)
    numerator, denominator = (numerator, denominator)
    total_numerator = numerator[0:per_block]
    total_denominator = denominator[0:per_block]
    for cycle_step in range(1, STEPS + 1):
        returned = passed_along(
            (
                numerator[cycle_step * per_block : (cycle_step + 1) * per_block],
                denominator[cycle_step * per_block : (cycle_step + 1) * per_block],
            ),
            "blk",
            -cycle_step,
        )
        total_numerator = total_numerator + returned[0]
        total_denominator = total_denominator + returned[1]
    return (total_numerator, total_denominator, evidence)


def solution(mesh):
    return jax.shard_map(
        body,
        mesh=mesh,
        in_specs=(
            P("blk", None, "shell"),
            P("blk", None, "shell"),
            P("blk"),
            P("shell"),
            P("shell"),
            P(),
            P("blk"),
        ),
        out_specs=(P("blk", None, "shell"), P("blk", "shell"), P("blk")),
        check_vma=False,
    )
```

profile of v0, /device:TPU:0, one launch (start us, length us, event | category | flops | bytes accessed | tf_op | source)
XLA Modules:
  0.0 270.0 jit_solution(14560077631796628932)
XLA Ops:
  7.2 0.0 all-reduce.2.cloned.1.call-start
  7.2 1.8 fusion.25
  9.1 0.5 collective-permute-start
  9.6 1.0 select_reduce_fusion
  10.5 30.1 %negate_multiply_fusion = f32[512,4096]{1,0:T(8,128)} fusion(f32[4096]{0:T(1024)S(1)} %get-tuple-element.16, f32[4096]{0:T(1024)} %param.10, f32[512]{0:T(512)} %param.9), kind=kLoop, calls=%fused_computation.2 | loop fusion | flops 8388608 | bytes 8423424 | tf_op jit(solution)/shard_map/mul | solution.py:26
  40.6 0.0 copy-start.2
  40.6 0.0 copy-start.3
  40.7 0.0 collective-permute-done
  40.7 2.7 collective-permute-start.1
  43.3 12.1 %multiply_convert_fusion = bf16[512,2,4096]{2,1,0:T(2,128)(2,1)} fusion(bf16[512,2,4096]{2,1,0:T(2,128)(2,1)} %param.7, f32[512,4096]{1,0:T(8,128)} %negate_multiply_fusion), kind=kLoop, calls=%fused_computation | loop fusion | flops 12582912 | bytes 25165824 | tf_op jit(solution)/shard_map/convert_element_type | solution.py:26
  55.5 0.1 constant_dynamic-update-slice_fusion.1
  55.6 2.6 collective-permute-done.1
  58.2 0.0 slice-start
  58.2 0.1 constant_dynamic-update-slice_fusion
  58.3 0.0 copy-done.2
  58.3 0.0 copy-done.3
  58.3 0.0 slice-start.1
  58.3 43.7 %fusion.5 = f32[192,512]{1,0:T(8,128)S(1)} fusion(f32[4096]{0:T(1024)S(1)} %get-tuple-element.15, f32[4096]{0:T(1024)S(1)} %copy-done.2, f32[512]{0:T(512)S(1)} %copy-done.3, bf16[192,2,4096]{2,0,1:T(8,128)(2,1)S(1)} %constant_dynamic-update-slice_fusion), kind=kOutput, calls=%fused_computation.9 | convolution fusion | flops 820510720 | bytes 3573760 | tf_op jit(solution)/shard_map/rp,ip->ri/dot_general | solution.py:38
  102.1 0.0 slice-done
  102.1 0.0 slice-done.1
  102.1 10.1 %fusion.14 = f32[192,512]{1,0:T(8,128)} fusion(f32[192,512]{1,0:T(8,128)S(1)} %fusion.5, bf16[192,2,4096]{2,0,1:T(8,128)(2,1)S(1)} %constant_dynamic-update-slice_fusion, bf16[512,2,4096]{2,1,0:T(2,128)(2,1)S(1)} %bitcast.15), kind=kOutput, calls=%fused_computation.17 | convolution fusion | flops 1610711040 | bytes 12320768 | tf_op jit(solution)/shard_map/rkp,ikp->ri/dot_general | solution.py:37
  112.2 0.0 all-reduce.2.cloned.1.call-update
  112.8 24.2 %all-reduce.2.cloned.1.call-done = f32[192,512]{1,0:T(8,128)} async-done(((f32[192,512]{1,0:T(8,128)}), f32[192,512]{1,0:T(8,128)}) %all-reduce.2.cloned.1.call-update) | async-done | bytes 393232 | tf_op jit(solution)/shard_map/psum | solution.py:42
  137.1 1.0 reduce_max.9
  138.1 1.1 exponential_reduce_fusion
  139.2 0.0 copy-start.1
  139.2 13.3 %fusion = f32[192,2,4096]{2,0,1:T(8,128)S(1)} fusion(bf16[512,2,4096]{2,1,0:T(2,128)(2,1)} %multiply_convert_fusion, f32[192,512]{1,0:T(8,128)} %all-reduce.2.cloned.1.call-done, f32[512]{0:T(512)S(1)} %add_select_fusion, pred[512]{0:T(512)(128)(4,1)S(1)} %iota_compare_fusion.1), kind=kOutput, calls=%fused_computation.4 | convolution fusion | flops 1610907648 | bytes 15075840 | tf_op jit(solution)/shard_map/ri,ikp->rkp/dot_general | solution.py:50
  152.5 0.0 copy-start
  152.6 0.4 fusion.23
  153.0 4.3 %collective-permute-start.3 = (f32[64,2,4096]{2,0,1:T(8,128)S(1)}, f32[64,2,4096]{2,0,1:T(8,128)S(1)}, u32[]{:S(2)}, u32[]{:S(2)}) collective-permute-start(f32[64,2,4096]{2,0,1:T(8,128)S(1)} %get-tuple-element.10), channel_id=1, source_target_pairs={{0,28},{2,30},{4,0},{6,2},{8,4},{10,6},{12,8},{14,10},{16,12},{18,... | collective-permute-start | bytes 6291464 | tf_op jit(solution)/shard_map/ppermute | solution.py:12
  157.3 0.0 collective-permute-start.2
  157.3 0.0 copy-done.1
  157.3 0.0 copy-done
  157.3 29.5 %fusion.4 = f32[192,4096]{1,0:T(8,128)S(1)} fusion(f32[4096]{0:T(1024)S(1)} %get-tuple-element.15, f32[4096]{0:T(1024)S(1)} %copy-done.2, f32[512]{0:T(512)S(1)} %copy-done.3, f32[192,512]{1,0:T(8,128)S(1)} %copy-done, f32[512]{0:T(512)S(1)} %add_select_fusion, pred[512]{0:T(512)(128)(4,1)S(1)} %iota_compare_fusion.1), kind=kOutput, calls=%fused_computation.8 | convolution fusion | flops 816087040 | bytes 3576320 | tf_op jit(solution)/shard_map/ri,ip->rp/dot_general | solution.py:51
  186.8 0.2 fusion.24
  187.0 1.2 collective-permute-start.5
  188.2 0.7 collective-permute-start.4
  188.8 58.3 %collective-permute-done.5 = f32[64,4096]{1,0:T(8,128)S(1)} collective-permute-done((f32[64,4096]{1,0:T(8,128)S(1)}, f32[64,4096]{1,0:T(8,128)S(1)}, u32[]{:S(2)}, u32[]{:S(2)}) %collective-permute-start.5) | collective-permute-done | bytes 1048608 | tf_op jit(solution)/shard_map/ppermute | solution.py:12
  247.1 11.2 %collective-permute-done.4 = f32[64,4096]{1,0:T(8,128)S(1)} collective-permute-done((f32[64,4096]{1,0:T(8,128)S(1)}, f32[64,4096]{1,0:T(8,128)S(1)}, u32[]{:S(2)}, u32[]{:S(2)}) %collective-permute-start.4) | collective-permute-done | bytes 1048608 | tf_op jit(solution)/shard_map/ppermute | solution.py:12
  258.4 1.2 fusion.17
  259.5 0.0 collective-permute-done.3
  259.6 0.0 collective-permute-done.2
  259.6 0.4 fusion.6
  260.0 2.9 %copy.19 = f32[64,2,4096]{2,1,0:T(2,128)} copy(f32[64,2,4096]{2,0,1:T(8,128)S(1)} %fusion.6) | data formatting | bytes 4194304
  (4 shorter events, 0.0 us)
Async XLA Ops:
  7.2 129.9 %all-reduce.2.cloned.1.call-start = ((), (), s32[]{:S(2)}) async-start(), calls=%async_computation | async-start | bytes 786432 | tf_op jit(solution)/shard_map/psum | solution.py:42
  9.1 31.6 %collective-permute-start = (bf16[64,2,4096]{2,0,1:T(8,128)(2,1)S(1)}, bf16[64,2,4096]{2,0,1:T(8,128)(2,1)S(1)}, u32[]{:S(2)}, u32[]{:S(2)}) collective-permute-start(bf16[64,2,4096]{2,0,1:T(8,128)(2,1)S(1)} %get-tuple-element.13), channel_id=1, source_target_pairs={{0,2},{2,4},{4,6},{6,8},{8,10},{10,12},{12,14},{14,16},{16,18},{18... | collective-permute-start | bytes 3145736 | tf_op jit(solution)/shard_map/ppermute | solution.py:12
  40.6 17.7 %copy-start.2 = (f32[4096]{0:T(1024)S(1)}, f32[4096]{0:T(1024)}, u32[]{:S(2)}) copy-start(f32[4096]{0:T(1024)} %param.10) | copy-start | bytes 49156
  40.6 17.7 %copy-start.3 = (f32[512]{0:T(512)S(1)}, f32[512]{0:T(512)}, u32[]{:S(2)}) copy-start(f32[512]{0:T(512)} %param.9) | copy-start | bytes 6148
  40.7 17.5 %collective-permute-start.1 = (bf16[64,2,4096]{2,0,1:T(8,128)(2,1)S(1)}, bf16[64,2,4096]{2,0,1:T(8,128)(2,1)S(1)}, u32[]{:S(2)}, u32[]{:S(2)}) collective-permute-start(bf16[64,2,4096]{2,0,1:T(8,128)(2,1)S(1)} %collective-permute-done), channel_id=1, source_target_pairs={{0,2},{2,4},{4,6},{6,8},{8,10},{10,12},{12,14},{14,16},{16,18},{18... | collective-permute-start | bytes 3145736 | tf_op jit(solution)/shard_map/ppermute | solution.py:12
  58.2 43.9 %slice-start = ((s8[8388608]{0:T(1024)(128)(4,1)}), s8[4194304]{0:T(1024)(128)(4,1)S(1)}, s32[]{:S(2)}) async-start(s8[8388608]{0:T(1024)(128)(4,1)} %bitcast.14), calls=%async_computation.1 | async-start | bytes 8388608
  58.3 43.8 %slice-start.1 = ((s8[8388608]{0:T(1024)(128)(4,1)}), s8[4194304]{0:T(1024)(128)(4,1)S(1)}, s32[]{:S(2)}) async-start(s8[8388608]{0:T(1024)(128)(4,1)} %bitcast.14), calls=%async_computation.2 | async-start | bytes 8388608
  139.2 18.1 %copy-start.1 = (f32[512]{0:T(512)}, f32[512]{0:T(512)S(1)}, u32[]{:S(2)}) copy-start(f32[512]{0:T(512)S(1)} %add_select_fusion) | copy-start | bytes 6148
  152.5 4.8 %copy-start = (f32[192,512]{1,0:T(8,128)S(1)}, f32[192,512]{1,0:T(8,128)}, u32[]{:S(2)}) copy-start(f32[192,512]{1,0:T(8,128)} %all-reduce.2.cloned.1.call-done) | copy-start | bytes 1179652
  153.0 106.5 %collective-permute-start.3 = (f32[64,2,4096]{2,0,1:T(8,128)S(1)}, f32[64,2,4096]{2,0,1:T(8,128)S(1)}, u32[]{:S(2)}, u32[]{:S(2)}) collective-permute-start(f32[64,2,4096]{2,0,1:T(8,128)S(1)} %get-tuple-element.10), channel_id=1, source_target_pairs={{0,28},{2,30},{4,0},{6,2},{8,4},{10,6},{12,8},{14,10},{16,12},{18,... | collective-permute-start | bytes 6291464 | tf_op jit(solution)/shard_map/ppermute | solution.py:12
  157.3 102.3 %collective-permute-start.2 = (f32[64,2,4096]{2,0,1:T(8,128)S(1)}, f32[64,2,4096]{2,0,1:T(8,128)S(1)}, u32[]{:S(2)}, u32[]{:S(2)}) collective-permute-start(f32[64,2,4096]{2,0,1:T(8,128)S(1)} %get-tuple-element.9), channel_id=1, source_target_pairs={{0,30},{2,0},{4,2},{6,4},{8,6},{10,8},{12,10},{14,12},{16,14},{18,... | collective-permute-start | bytes 6291464 | tf_op jit(solution)/shard_map/ppermute | solution.py:12
  187.0 60.2 %collective-permute-start.5 = (f32[64,4096]{1,0:T(8,128)S(1)}, f32[64,4096]{1,0:T(8,128)S(1)}, u32[]{:S(2)}, u32[]{:S(2)}) collective-permute-start(f32[64,4096]{1,0:T(8,128)S(1)} %get-tuple-element.12), channel_id=1, source_target_pairs={{0,28},{2,30},{4,0},{6,2},{8,4},{10,6},{12,8},{14,10},{16,12},{18,... | collective-permute-start | bytes 3145736 | tf_op jit(solution)/shard_map/ppermute | solution.py:12
  188.2 70.2 %collective-permute-start.4 = (f32[64,4096]{1,0:T(8,128)S(1)}, f32[64,4096]{1,0:T(8,128)S(1)}, u32[]{:S(2)}, u32[]{:S(2)}) collective-permute-start(f32[64,4096]{1,0:T(8,128)S(1)} %get-tuple-element.11), channel_id=1, source_target_pairs={{0,30},{2,0},{4,2},{6,4},{8,6},{10,8},{12,10},{14,12},{16,14},{18,... | collective-permute-start | bytes 3145736 | tf_op jit(solution)/shard_map/ppermute | solution.py:12
Sparse Core Ops, SparseCore 0:
  112.3 24.7 all-reduce.1
where the time goes:
time: 275 us; the launch traced here: 270 us
  matrix products  96.6 us (35%)
  waiting for transfers between devices  96.4 us (35%)
  other arithmetic  46.9 us (17%)
  between operations  15 us (5%)
  starting transfers between devices  9.38 us (3%)
  local copies, waits for them, and re-layouts  5.58 us (2%)
    ppermute x6, waiting for transfers between devices, passed_along(): return lax.ppermute(value, axis, pairs)  72.2 us
    dot_general x1, matrix products, body(): jnp.einsum('rp,ip->ri', reference_power, envelope, preferred_element_type...  43.7 us
    mul x1, other arithmetic, body(): contrast * weight  30.1 us
    dot_general x1, matrix products, body(): jnp.einsum('ri,ip->rp', posterior, envelope, preferred_element_type=jnp.f...  29.5 us
    psum x1, waiting for transfers between devices, body(): scores = lax.psum(partial_scores, 'shell')  24.2 us
    dot_general x1, matrix products, body(): jnp.einsum('ri,ikp->rkp', posterior, filtered, preferred_element_type=jnp...  13.3 us
    convert_element_type x1, other arithmetic, body(): (images.astype(jnp.float32) * (contrast * weight)[:, None, :]).astype(jnp...  12.1 us
    dot_general x1, matrix products, body(): jnp.einsum('rkp,ikp->ri', visited, filtered, preferred_element_type=jnp.f...  10.1 us
  transfers between devices with their start and end apart: 7, of which 4 were waited for; matrix products, arithmetic and copies ran while one was open for 27% of the time, Pallas kernels for 0%

commit v1 on v0

v1 whole, which is shorter than its diff:
```python
import math

import jax
import jax.numpy as jnp
from jax import lax
from jax.sharding import PartitionSpec as P

CHUNKS = 2
TURN = 2.0 * math.pi


def passed_along(value, axis, steps):
    count = lax.axis_size(axis)
    pairs = [(source, (source + steps) % count) for source in range(count)]
    return lax.ppermute(value, axis, pairs)


def minus_sine(defocus, turns):
    shifted = defocus[:, None] * turns[None, :] + (0.1 / TURN - 0.25)
    rest = shifted - jnp.round(shifted)
    y = 0.25 - jnp.abs(rest)
    square = y * y
    coefficients = [TURN ** k / math.factorial(k) * (1 if k % 4 == 3 else -1) for k in (1, 3, 5, 7, 9, 11)]
    value = jnp.full_like(square, coefficients[-1])
    for coefficient in coefficients[-2::-1]:
        value = value * square + coefficient
    return value * y


def body(images, references, defocus, frequency_squared, shell_index, noise_power, live_count):
    capacity = images.shape[0]
    per_block, _, pixels = references.shape
    shells = noise_power.shape[0]
    first = passed_along(references, "blk", 1)
    second = passed_along(first, "blk", 1)
    defocus_1 = passed_along(defocus, "blk", -1)
    defocus_2 = passed_along(defocus, "blk", -2)
    lookup = jnp.where(
        jnp.arange(shells, dtype=jnp.int32)[:, None] == shell_index[None, :],
        noise_power[:, None],
        0.0,
    )
    weight = 1.0 / jnp.sum(lookup, axis=0)
    half_weight = 0.5 * weight
    turns = frequency_squared * (1.0 / TURN)
    contrast = minus_sine(defocus, turns)
    filtered = (images.astype(jnp.float32) * (contrast * weight)[:, None, :]).astype(jnp.bfloat16)
    envelope = (contrast * contrast * half_weight).astype(jnp.bfloat16)
    filtered, envelope = lax.optimization_barrier((filtered, envelope))

    def envelope_of(values):
        other = minus_sine(values, turns)
        return (other * other * half_weight).astype(jnp.bfloat16)

    def partial(block):
        wide = block.astype(jnp.float32)
        power = (jnp.square(wide[:, 0]) + jnp.square(wide[:, 1])).astype(jnp.bfloat16)
        crossed = jnp.einsum("rkp,ikp->ri", block, filtered, preferred_element_type=jnp.float32)
        quadratic = jnp.einsum("rp,ip->ri", power, envelope, preferred_element_type=jnp.float32)
        return crossed - quadratic

    parts = []
    for block in (references, first, second):
        mine = partial(block)
        parts.append(mine + passed_along(mine, "shell", 1))
    scores = jnp.concatenate(parts, 0)
    live_slots = jnp.arange(capacity, dtype=jnp.int32) < live_count[0]
    highest = jnp.max(scores, axis=0)
    summed = jnp.sum(jnp.exp(scores - highest[None, :]), axis=0)
    evidence = jnp.where(live_slots, highest + jnp.log(summed), 0.0)
    posterior = jnp.where(live_slots[None, :], jnp.exp(scores - evidence[None, :]), 0.0).astype(
        jnp.bfloat16
    )
    here, back_1, back_2 = [posterior[s * per_block : (s + 1) * per_block] for s in range(3)]
    width = pixels // CHUNKS
    columns = [slice(c * width, (c + 1) * width) for c in range(CHUNKS)]

    def sums(rows, cut):
        return jnp.einsum(
            "ri,ikp->rkp", rows, filtered[:, :, cut], preferred_element_type=jnp.float32
        )

    returned_1 = passed_along(back_1, "blk", -1)
    returned_2 = passed_along(back_2, "blk", -2)
    farther = [passed_along(sums(back_2, cut).astype(jnp.bfloat16), "blk", -1) for cut in columns]
    nearer = [
        passed_along((sums(back_1, cut) + got.astype(jnp.float32)).astype(jnp.bfloat16), "blk", -1)
        for cut, got in zip(columns, farther)
    ]
    numerator = jnp.concatenate(
        [sums(here, cut) + got.astype(jnp.float32) for cut, got in zip(columns, nearer)], 2
    )
    denominator = sum(
        jnp.einsum("ri,ip->rp", rows, values, preferred_element_type=jnp.float32)
        for rows, values in (
            (here, envelope),
            (returned_1, envelope_of(defocus_1)),
            (returned_2, envelope_of(defocus_2)),
        )
    )
    return (numerator, denominator, evidence)


def solution(mesh):
    return jax.shard_map(
        body,
        mesh=mesh,
        in_specs=(
            P("blk", None, "shell"),
            P("blk", None, "shell"),
            P("blk"),
            P("shell"),
            P("shell"),
            P(),
            P("blk"),
        ),
        out_specs=(P("blk", None, "shell"), P("blk", "shell"), P("blk")),
        check_vma=False,
    )
```

time: 275 us -> 93 us (0.34); the launches traced: 270 us -> 92.6 us
  waiting for transfers between devices: 96.4 us -> 17.9 us
  matrix products: 96.6 us -> 31 us
  other arithmetic: 46.9 us -> 18.4 us
  between operations: 15 us -> 1.54 us
  starting transfers between devices: 9.38 us -> 20.7 us
    dot_general x4 -> x15, matrix products: 96.6 us -> 31 us  [the longest x3 13.7 us: body(): jnp.einsum('ri,ip->rp', rows, values, preferred_element_type=jnp.float32)]
    ppermute x6 -> x13, waiting for transfers between devices: 72.2 us -> 17.9 us  [passed_along(): return lax.ppermute(value, axis, pairs)]
    mul x2 -> x1, other arithmetic: 30.1 us -> 0.73 us  [body(): half_weight = 0.5 * weight]
    psum x1 -> x0, waiting for transfers between devices: 24.2 us -> none  [body(): scores = lax.psum(partial_scores, 'shell')]
    ppermute x6 -> x13, starting transfers between devices: 9.34 us -> 20.7 us  [passed_along(): return lax.ppermute(value, axis, pairs)]
    convert_element_type x0 -> x5, other arithmetic: none -> 9.51 us  [the longest x1 6.93 us: body(): envelope = (contrast * contrast * half_weight).astype(jnp.bfloat16)]
    convert_element_type x1, other arithmetic: 12.1 us -> 6.88 us  [body(): (images.astype(jnp.float32) * (contrast * weight)[:, None, :]).astype(jnp...]
  transfers between devices with their start and end apart: 7 -> 13, of which waited for: 4 -> 5; matrix products, arithmetic and copies ran while one was open for 27% -> 50% of each run, Pallas kernels for 0% -> 0%
where the time goes in v1:
time: 93 us; the launch traced here: 92.6 us
  matrix products  31 us (33%)
  starting transfers between devices  20.7 us (22%)
  other arithmetic  18.4 us (20%)
  waiting for transfers between devices  17.9 us (19%)
  local copies, waits for them, and re-layouts  2.98 us (3%)
  between operations  1.54 us (2%)
    ppermute x13, starting transfers between devices, passed_along(): return lax.ppermute(value, axis, pairs)  20.7 us
    ppermute x13, waiting for transfers between devices, passed_along(): return lax.ppermute(value, axis, pairs)  17.9 us
    dot_general x3, matrix products, body(): jnp.einsum('ri,ip->rp', rows, values, preferred_element_type=jnp.float32)  13.7 us
    dot_general x3, matrix products, partial(): jnp.einsum('rkp,ikp->ri', block, filtered, preferred_element_type=jnp.flo...  8.02 us
    convert_element_type x1, other arithmetic, body(): envelope = (contrast * contrast * half_weight).astype(jnp.bfloat16)  6.93 us
    convert_element_type x1, other arithmetic, body(): (images.astype(jnp.float32) * (contrast * weight)[:, None, :]).astype(jnp...  6.88 us
    dot_general x6, matrix products, sums(): jnp.einsum('ri,ikp->rkp', rows, filtered[:, :, cut], preferred_element_ty...  5.06 us
    dot_general x3, matrix products, partial(): jnp.einsum('rp,ip->ri', power, envelope, preferred_element_type=jnp.float32)  4.24 us
  transfers between devices with their start and end apart: 13, of which 5 were waited for; matrix products, arithmetic and copies ran while one was open for 50% of the time, Pallas kernels for 0%

profile of v1, /device:TPU:0, one launch (start us, length us, event | category | flops | bytes accessed | tf_op | source)
XLA Modules:
  0.0 92.6 jit_solution(6123559784920563140)
XLA Ops:
  0.6 0.0 slice-start
  0.6 2.1 %copy_convert_fusion = (f32[64,2,4096]{2,0,1:T(8,128)S(1)}, bf16[64,2,4096]{2,0,1:T(8,128)(2,1)S(1)}) fusion(bf16[64,2,4096]{2,1,0:T(2,128)(2,1)} %param.8), kind=kLoop, calls=%fused_computation.138 | loop fusion | flops 524288 | bytes 4194304 | tf_op jit(solution)/shard_map/convert_element_type | solution.py:56
  2.7 0.5 collective-permute-start.1
  3.3 1.0 %select_reduce_fusion = f32[4096]{0:T(1024)S(1)} fusion(f32[64]{0:T(128)} %param.12, s32[4096]{0:T(1024)} %param.11), kind=kLoop, calls=%fused_computation.92 | loop fusion | flops 782336 | bytes 33024 | tf_op jit(solution)/shard_map/reduce_sum | solution.py:43
  4.2 0.7 broadcast_multiply_fusion.1
  5.0 0.0 slice-start.1
  5.0 6.9 %multiply_convert_fusion.3 = (bf16[512,4096]{1,0:T(8,128)(2,1)S(1)}, f32[512,4096]{1,0:T(8,128)S(1)}) fusion(f32[4096]{0:T(1024)S(1)} %get-tuple-element.28, f32[4096]{0:T(1024)S(1)} %get-tuple-element.30, f32[512]{0:T(512)} %param.9, f32[4096]{0:T(1024)S(1)} %get-tuple-element.29), kind=kLoop, calls=%fused_computation.24 | loop fusion | flops 46137344 | bytes 12634112 | tf_op jit(solution)/shard_map/convert_element_type | solution.py:48
  11.9 0.0 slice-done
  11.9 0.0 slice-done.1
  11.9 0.0 copy-start
  11.9 6.9 %multiply_convert_fusion = bf16[512,2,4096]{2,0,1:T(8,128)(2,1)S(1)} fusion(bf16[512,2,4096]{2,1,0:T(2,128)(2,1)S(1)} %bitcast.63, f32[512,4096]{1,0:T(8,128)S(1)} %get-tuple-element.27), kind=kLoop, calls=%fused_computation | loop fusion | flops 12582912 | bytes 25165824 | tf_op jit(solution)/shard_map/convert_element_type | solution.py:47
  18.8 0.0 copy-start.2
  18.8 0.0 copy-done
  18.8 2.7 %convolution_bitcast_fusion.2 = f32[64,512]{1,0:T(8,128)S(1)} fusion(bf16[512,2,4096]{2,0,1:T(8,128)(2,1)S(1)} %multiply_convert_fusion, bf16[64,2,4096]{2,1,0:T(2,128)(2,1)S(1)} %copy-done), kind=kOutput, calls=%fused_computation.75 | convolution fusion | flops 536870912 | bytes 9568256 | tf_op jit(solution)/shard_map/rkp,ikp->ri/dot_general | solution.py:58
  21.5 1.4 %convolution_subtract_fusion = f32[64,512]{1,0:T(8,128)S(1)} fusion(f32[64,512]{1,0:T(8,128)S(1)} %convolution_bitcast_fusion.2, bf16[512,4096]{1,0:T(8,128)(2,1)S(1)} %get-tuple-element.6, f32[64,2,4096]{2,0,1:T(8,128)S(1)} %get-tuple-element.22), kind=kOutput, calls=%fused_computation.70 | convolution fusion | flops 269516800 | bytes 6553600 | tf_op jit(solution)/shard_map/rp,ip->ri/dot_general | solution.py:59
  22.9 2.6 %collective-permute-start = (f32[64,512]{1,0:T(8,128)S(1)}, f32[64,512]{1,0:T(8,128)S(1)}, u32[]{:S(2)}, u32[]{:S(2)}) collective-permute-start(f32[64,512]{1,0:T(8,128)S(1)} %convolution_subtract_fusion), channel_id=1, source_target_pairs={{0,1},{1,0},{2,3},{3,2},{4,5},{5,4},{6,7},{7,6},{8,9},{9,8},{10,11... | collective-permute-start | bytes 393224 | tf_op jit(solution)/shard_map/ppermute | solution.py:15
  25.5 0.0 copy-done.2
  25.5 4.1 %collective-permute-start.10 = (f32[512]{0:T(512)S(1)}, f32[512]{0:T(512)S(1)}, u32[]{:S(2)}, u32[]{:S(2)}) collective-permute-start(f32[512]{0:T(512)S(1)} %copy-done.2), channel_id=1, source_target_pairs={{0,30},{2,0},{4,2},{6,4},{8,6},{10,8},{12,10},{14,12},{16,14},{18,... | collective-permute-start | bytes 6152 | tf_op jit(solution)/shard_map/ppermute | solution.py:15
  29.6 1.9 %collective-permute-start.12 = (f32[512]{0:T(512)S(1)}, f32[512]{0:T(512)S(1)}, u32[]{:S(2)}, u32[]{:S(2)}) collective-permute-start(f32[512]{0:T(512)S(1)} %copy-done.2), channel_id=1, source_target_pairs={{0,28},{2,30},{4,0},{6,2},{8,4},{10,6},{12,8},{14,10},{16,12},{18,... | collective-permute-start | bytes 6152 | tf_op jit(solution)/shard_map/ppermute | solution.py:15
  32.2 0.0 collective-permute-done.1
  32.2 0.2 collective-permute-start.3
  32.4 0.0 collective-permute-done
  32.5 0.2 convert_element_type.75
  32.7 1.4 %fusion.64 = f32[64,512]{1,0:T(8,128)S(1)} fusion(bf16[512,4096]{1,0:T(8,128)(2,1)S(1)} %get-tuple-element.6, f32[64,2,4096]{2,0,1:T(8,128)S(1)} %convert_element_type.75), kind=kOutput, calls=%fused_computation.96 | convolution fusion | flops 269484032 | bytes 6422528 | tf_op jit(solution)/shard_map/rp,ip->ri/dot_general | solution.py:59
  34.1 2.7 %fusion.54 = f32[64,512]{1,0:T(8,128)S(1)} fusion(f32[64,512]{1,0:T(8,128)S(1)} %fusion.64, bf16[512,2,4096]{2,0,1:T(8,128)(2,1)S(1)} %multiply_convert_fusion, bf16[64,2,4096]{2,0,1:T(8,128)(2,1)S(1)} %collective-permute-done.1), kind=kOutput, calls=%fused_computation.74 | convolution fusion | flops 536903680 | bytes 9699328 | tf_op jit(solution)/shard_map/rkp,ikp->ri/dot_general | solution.py:58
  36.8 0.6 collective-permute-start.2
  37.4 12.0 %collective-permute-done.3 = bf16[64,2,4096]{2,0,1:T(8,128)(2,1)S(1)} collective-permute-done((bf16[64,2,4096]{2,0,1:T(8,128)(2,1)S(1)}, bf16[64,2,4096]{2,0,1:T(8,128)(2,1)S(1)}, u32[]{:S(2)}, u32[]{:S(2)}) %collective-permute-start.3) | collective-permute-done | bytes 1048608 | tf_op jit(solution)/shard_map/ppermute | solution.py:15
  49.3 0.2 convert_element_type.78
  49.5 1.4 %fusion.67 = f32[64,512]{1,0:T(8,128)S(1)} fusion(bf16[512,4096]{1,0:T(8,128)(2,1)S(1)} %get-tuple-element.6, f32[64,2,4096]{2,0,1:T(8,128)S(1)} %convert_element_type.78), kind=kOutput, calls=%fused_computation.98 | convolution fusion | flops 269484032 | bytes 6422528 | tf_op jit(solution)/shard_map/rp,ip->ri/dot_general | solution.py:59
  51.0 2.7 %fusion.53 = f32[64,512]{1,0:T(8,128)S(1)} fusion(f32[64,512]{1,0:T(8,128)S(1)} %fusion.67, bf16[512,2,4096]{2,0,1:T(8,128)(2,1)S(1)} %multiply_convert_fusion, bf16[64,2,4096]{2,0,1:T(8,128)(2,1)S(1)} %collective-permute-done.3), kind=kOutput, calls=%fused_computation.72 | convolution fusion | flops 536903680 | bytes 9699328 | tf_op jit(solution)/shard_map/rkp,ikp->ri/dot_general | solution.py:58
  53.7 0.6 collective-permute-start.4
  54.2 0.0 collective-permute-done.2
  54.3 4.4 %collective-permute-done.4 = f32[64,512]{1,0:T(8,128)S(1)} collective-permute-done((f32[64,512]{1,0:T(8,128)S(1)}, f32[64,512]{1,0:T(8,128)S(1)}, u32[]{:S(2)}, u32[]{:S(2)}) %collective-permute-start.4) | collective-permute-done | bytes 131104 | tf_op jit(solution)/shard_map/ppermute | solution.py:15
  58.7 0.1 exponential_reduce_fusion
  58.8 0.0 copy-start.1
  58.8 0.1 select_convert_fusion
  58.9 0.8 fusion.92
  59.8 0.8 fusion.47
  60.6 0.1 collective-permute-start.9
  60.7 0.8 fusion.50
  61.5 0.1 collective-permute-start.11
  61.7 0.2 collective-permute-start.5
  61.9 0.0 collective-permute-done.10
  61.9 0.3 collective-permute-start.7
  62.2 0.4 collective-permute-done.9
  62.6 5.9 %convolution_add_fusion.1 = f32[64,4096]{1,0:T(8,128)S(1)} fusion(f32[64,4096]{1,0:T(8,128)S(1)} %fusion.92, bf16[64,512]{1,0:T(8,128)(2,1)S(1)} %collective-permute-done.9, f32[512]{0:T(512)S(1)} %collective-permute-done.10, f32[4096]{0:T(1024)S(1)} %get-tuple-element.28, f32[4096]{0:T(1024)S(1)} %get-tuple-element.30), kind=kOutput, calls=%fused_computation.33 | convolution fusion | flops 312737792 | bytes 2197504 | tf_op jit(solution)/shard_map/ri,ip->rp/dot_general | solution.py:94
  68.5 0.0 copy-done.1
  68.5 1.0 %collective-permute-done.5 = bf16[64,2,2048]{2,0,1:T(8,128)(2,1)S(1)} collective-permute-done((bf16[64,2,2048]{2,0,1:T(8,128)(2,1)S(1)}, bf16[64,2,2048]{2,0,1:T(8,128)(2,1)S(1)}, u32[]{:S(2)}, u32[]{:S(2)}) %collective-permute-start.5) | collective-permute-done | bytes 524320 | tf_op jit(solution)/shard_map/ppermute | solution.py:15
  69.5 0.8 add_convert_fusion.1
  70.4 4.7 %collective-permute-start.6 = (bf16[64,2,2048]{2,0,1:T(8,128)(2,1)S(1)}, bf16[64,2,2048]{2,0,1:T(8,128)(2,1)S(1)}, u32[]{:S(2)}, u32[]{:S(2)}) collective-permute-start(bf16[64,2,2048]{2,0,1:T(8,128)(2,1)S(1)} %add_convert_fusion.1), channel_id=1, source_target_pairs={{0,30},{2,0},{4,2},{6,4},{8,6},{10,8},{12,10},{14,12},{16,14},{18,... | collective-permute-start | bytes 1572872 | tf_op jit(solution)/shard_map/ppermute | solution.py:15
  75.0 0.1 collective-permute-done.7
  75.1 0.8 add_convert_fusion
  76.0 4.9 %collective-permute-start.8 = (bf16[64,2,2048]{2,0,1:T(8,128)(2,1)S(1)}, bf16[64,2,2048]{2,0,1:T(8,128)(2,1)S(1)}, u32[]{:S(2)}, u32[]{:S(2)}) collective-permute-start(bf16[64,2,2048]{2,0,1:T(8,128)(2,1)S(1)} %add_convert_fusion), channel_id=1, source_target_pairs={{0,30},{2,0},{4,2},{6,4},{8,6},{10,8},{12,10},{14,12},{16,14},{18,... | collective-permute-start | bytes 1572872 | tf_op jit(solution)/shard_map/ppermute | solution.py:15
  80.9 0.0 collective-permute-done.12
  80.9 0.0 collective-permute-done.11
  80.9 6.9 %convolution_add_fusion = f32[64,4096]{1,0:T(8,128)} fusion(f32[64,4096]{1,0:T(8,128)S(1)} %convolution_add_fusion.1, bf16[64,512]{1,0:T(8,128)(2,1)S(1)} %collective-permute-done.11, f32[512]{0:T(512)S(1)} %collective-permute-done.12, f32[4096]{0:T(1024)S(1)} %get-tuple-element.28, f32[4096]{0:T(1024)S(1)} %get-tuple-element.30), kind=kOutput, calls=%fused_computation.32 | convolution fusion | flops 312737792 | bytes 2197504 | tf_op jit(solution)/shard_map/ri,ip->rp/dot_general | solution.py:94
  87.8 0.0 collective-permute-done.6
  87.8 0.8 convert_add_fusion.1
  88.7 0.0 collective-permute-done.8
  88.7 0.8 convert_add_fusion
  89.5 0.1 pad_maximum_fusion
  89.7 2.9 %copy.23 = f32[64,2,4096]{2,1,0:T(2,128)} copy(f32[64,2,4096]{2,0,1:T(8,128)S(1)} %pad_maximum_fusion) | data formatting | bytes 4194304
  (8 shorter events, 0.1 us)
Async XLA Ops:
  0.6 11.3 %slice-start = ((s8[8388608]{0:T(1024)(128)(4,1)}), s8[4194304]{0:T(1024)(128)(4,1)S(1)}, s32[]{:S(2)}) async-start(s8[8388608]{0:T(1024)(128)(4,1)} %bitcast.62), calls=%async_computation | async-start | bytes 8388608
  2.7 29.4 %collective-permute-start.1 = (bf16[64,2,4096]{2,0,1:T(8,128)(2,1)S(1)}, bf16[64,2,4096]{2,0,1:T(8,128)(2,1)S(1)}, u32[]{:S(2)}, u32[]{:S(2)}) collective-permute-start(bf16[64,2,4096]{2,0,1:T(8,128)(2,1)S(1)} %get-tuple-element.23), channel_id=1, source_target_pairs={{0,2},{2,4},{4,6},{6,8},{8,10},{10,12},{12,14},{14,16},{16,18},{18... | collective-permute-start | bytes 3145736 | tf_op jit(solution)/shard_map/ppermute | solution.py:15
  5.0 7.0 %slice-start.1 = ((s8[8388608]{0:T(1024)(128)(4,1)}), s8[4194304]{0:T(1024)(128)(4,1)S(1)}, s32[]{:S(2)}) async-start(s8[8388608]{0:T(1024)(128)(4,1)} %bitcast.62), calls=%async_computation.1 | async-start | bytes 8388608
  11.9 6.9 %copy-start = (bf16[64,2,4096]{2,1,0:T(2,128)(2,1)S(1)}, bf16[64,2,4096]{2,1,0:T(2,128)(2,1)}, u32[]{:S(2)}) copy-start(bf16[64,2,4096]{2,1,0:T(2,128)(2,1)} %param.8) | copy-start | bytes 3145732
  18.8 6.7 %copy-start.2 = (f32[512]{0:T(512)S(1)}, f32[512]{0:T(512)}, u32[]{:S(2)}) copy-start(f32[512]{0:T(512)} %param.9) | copy-start | bytes 6148
  22.9 9.5 %collective-permute-start = (f32[64,512]{1,0:T(8,128)S(1)}, f32[64,512]{1,0:T(8,128)S(1)}, u32[]{:S(2)}, u32[]{:S(2)}) collective-permute-start(f32[64,512]{1,0:T(8,128)S(1)} %convolution_subtract_fusion), channel_id=1, source_target_pairs={{0,1},{1,0},{2,3},{3,2},{4,5},{5,4},{6,7},{7,6},{8,9},{9,8},{10,11... | collective-permute-start | bytes 393224 | tf_op jit(solution)/shard_map/ppermute | solution.py:15
  25.5 36.4 %collective-permute-start.10 = (f32[512]{0:T(512)S(1)}, f32[512]{0:T(512)S(1)}, u32[]{:S(2)}, u32[]{:S(2)}) collective-permute-start(f32[512]{0:T(512)S(1)} %copy-done.2), channel_id=1, source_target_pairs={{0,30},{2,0},{4,2},{6,4},{8,6},{10,8},{12,10},{14,12},{16,14},{18,... | collective-permute-start | bytes 6152 | tf_op jit(solution)/shard_map/ppermute | solution.py:15
  29.6 51.3 %collective-permute-start.12 = (f32[512]{0:T(512)S(1)}, f32[512]{0:T(512)S(1)}, u32[]{:S(2)}, u32[]{:S(2)}) collective-permute-start(f32[512]{0:T(512)S(1)} %copy-done.2), channel_id=1, source_target_pairs={{0,28},{2,30},{4,0},{6,2},{8,4},{10,6},{12,8},{14,10},{16,12},{18,... | collective-permute-start | bytes 6152 | tf_op jit(solution)/shard_map/ppermute | solution.py:15
  32.2 17.2 %collective-permute-start.3 = (bf16[64,2,4096]{2,0,1:T(8,128)(2,1)S(1)}, bf16[64,2,4096]{2,0,1:T(8,128)(2,1)S(1)}, u32[]{:S(2)}, u32[]{:S(2)}) collective-permute-start(bf16[64,2,4096]{2,0,1:T(8,128)(2,1)S(1)} %collective-permute-done.1), channel_id=1, source_target_pairs={{0,2},{2,4},{4,6},{6,8},{8,10},{10,12},{12,14},{14,16},{16,18},{18... | collective-permute-start | bytes 3145736 | tf_op jit(solution)/shard_map/ppermute | solution.py:15
  36.8 17.5 %collective-permute-start.2 = (f32[64,512]{1,0:T(8,128)S(1)}, f32[64,512]{1,0:T(8,128)S(1)}, u32[]{:S(2)}, u32[]{:S(2)}) collective-permute-start(f32[64,512]{1,0:T(8,128)S(1)} %fusion.54), channel_id=1, source_target_pairs={{0,1},{1,0},{2,3},{3,2},{4,5},{5,4},{6,7},{7,6},{8,9},{9,8},{10,11... | collective-permute-start | bytes 393224 | tf_op jit(solution)/shard_map/ppermute | solution.py:15
  53.7 5.0 %collective-permute-start.4 = (f32[64,512]{1,0:T(8,128)S(1)}, f32[64,512]{1,0:T(8,128)S(1)}, u32[]{:S(2)}, u32[]{:S(2)}) collective-permute-start(f32[64,512]{1,0:T(8,128)S(1)} %fusion.53), channel_id=1, source_target_pairs={{0,1},{1,0},{2,3},{3,2},{4,5},{5,4},{6,7},{7,6},{8,9},{9,8},{10,11... | collective-permute-start | bytes 393224 | tf_op jit(solution)/shard_map/ppermute | solution.py:15
  58.8 9.7 %copy-start.1 = (f32[512]{0:T(512)}, f32[512]{0:T(512)S(1)}, u32[]{:S(2)}) copy-start(f32[512]{0:T(512)S(1)} %add_select_fusion) | copy-start | bytes 6148
  60.6 2.0 %collective-permute-start.9 = (bf16[64,512]{1,0:T(8,128)(2,1)S(1)}, bf16[64,512]{1,0:T(8,128)(2,1)S(1)}, u32[]{:S(2)}, u32[]{:S(2)}) collective-permute-start(bf16[64,512]{1,0:T(8,128)(2,1)S(1)} %get-tuple-element.25), channel_id=1, source_target_pairs={{0,30},{2,0},{4,2},{6,4},{8,6},{10,8},{12,10},{14,12},{16,14},{18,... | collective-permute-start | bytes 196616 | tf_op jit(solution)/shard_map/ppermute | solution.py:15
  61.5 19.4 %collective-permute-start.11 = (bf16[64,512]{1,0:T(8,128)(2,1)S(1)}, bf16[64,512]{1,0:T(8,128)(2,1)S(1)}, u32[]{:S(2)}, u32[]{:S(2)}) collective-permute-start(bf16[64,512]{1,0:T(8,128)(2,1)S(1)} %get-tuple-element.24), channel_id=1, source_target_pairs={{0,28},{2,30},{4,0},{6,2},{8,4},{10,6},{12,8},{14,10},{16,12},{18,... | collective-permute-start | bytes 196616 | tf_op jit(solution)/shard_map/ppermute | solution.py:15
  61.7 7.8 %collective-permute-start.5 = (bf16[64,2,2048]{2,0,1:T(8,128)(2,1)S(1)}, bf16[64,2,2048]{2,0,1:T(8,128)(2,1)S(1)}, u32[]{:S(2)}, u32[]{:S(2)}) collective-permute-start(bf16[64,2,2048]{2,0,1:T(8,128)(2,1)S(1)} %fusion.47), channel_id=1, source_target_pairs={{0,30},{2,0},{4,2},{6,4},{8,6},{10,8},{12,10},{14,12},{16,14},{18,... | collective-permute-start | bytes 1572872 | tf_op jit(solution)/shard_map/ppermute | solution.py:15
  61.9 13.3 %collective-permute-start.7 = (bf16[64,2,2048]{2,0,1:T(8,128)(2,1)S(1)}, bf16[64,2,2048]{2,0,1:T(8,128)(2,1)S(1)}, u32[]{:S(2)}, u32[]{:S(2)}) collective-permute-start(bf16[64,2,2048]{2,0,1:T(8,128)(2,1)S(1)} %fusion.50), channel_id=1, source_target_pairs={{0,30},{2,0},{4,2},{6,4},{8,6},{10,8},{12,10},{14,12},{16,14},{18,... | collective-permute-start | bytes 1572872 | tf_op jit(solution)/shard_map/ppermute | solution.py:15
  70.4 17.4 %collective-permute-start.6 = (bf16[64,2,2048]{2,0,1:T(8,128)(2,1)S(1)}, bf16[64,2,2048]{2,0,1:T(8,128)(2,1)S(1)}, u32[]{:S(2)}, u32[]{:S(2)}) collective-permute-start(bf16[64,2,2048]{2,0,1:T(8,128)(2,1)S(1)} %add_convert_fusion.1), channel_id=1, source_target_pairs={{0,30},{2,0},{4,2},{6,4},{8,6},{10,8},{12,10},{14,12},{16,14},{18,... | collective-permute-start | bytes 1572872 | tf_op jit(solution)/shard_map/ppermute | solution.py:15
  76.0 12.7 %collective-permute-start.8 = (bf16[64,2,2048]{2,0,1:T(8,128)(2,1)S(1)}, bf16[64,2,2048]{2,0,1:T(8,128)(2,1)S(1)}, u32[]{:S(2)}, u32[]{:S(2)}) collective-permute-start(bf16[64,2,2048]{2,0,1:T(8,128)(2,1)S(1)} %add_convert_fusion), channel_id=1, source_target_pairs={{0,30},{2,0},{4,2},{6,4},{8,6},{10,8},{12,10},{14,12},{16,14},{18,... | collective-permute-start | bytes 1572872 | tf_op jit(solution)/shard_map/ppermute | solution.py:15

commit v2 on v1

--- a/solution.py
+++ b/solution.py
@@ -32,7 +32,6 @@
     per_block, _, pixels = references.shape
     shells = noise_power.shape[0]
     first = passed_along(references, "blk", 1)
-    second = passed_along(first, "blk", 1)
     defocus_1 = passed_along(defocus, "blk", -1)
     defocus_2 = passed_along(defocus, "blk", -2)
     lookup = jnp.where(
@@ -43,25 +42,33 @@
     weight = 1.0 / jnp.sum(lookup, axis=0)
     half_weight = 0.5 * weight
     turns = frequency_squared * (1.0 / TURN)
-    contrast = minus_sine(defocus, turns)
-    filtered = (images.astype(jnp.float32) * (contrast * weight)[:, None, :]).astype(jnp.bfloat16)
-    envelope = (contrast * contrast * half_weight).astype(jnp.bfloat16)
-    filtered, envelope = lax.optimization_barrier((filtered, envelope))
+    width = pixels // CHUNKS
+    columns = [slice(c * width, (c + 1) * width) for c in range(CHUNKS)]
 
     def envelope_of(values):
         other = minus_sine(values, turns)
         return (other * other * half_weight).astype(jnp.bfloat16)
 
-    def partial(block):
+    contrast = minus_sine(defocus, turns)
+    filtered = (images.astype(jnp.float32) * (contrast * weight)[:, None, :]).astype(jnp.bfloat16)
+    envelope = (contrast * contrast * half_weight).astype(jnp.bfloat16)
+    first, envelope, filtered = lax.optimization_barrier((first, envelope, filtered))
+    second = [passed_along(first[:, :, cut], "blk", 1) for cut in columns]
+
+    def partial(block, cut):
         wide = block.astype(jnp.float32)
         power = (jnp.square(wide[:, 0]) + jnp.square(wide[:, 1])).astype(jnp.bfloat16)
-        crossed = jnp.einsum("rkp,ikp->ri", block, filtered, preferred_element_type=jnp.float32)
-        quadratic = jnp.einsum("rp,ip->ri", power, envelope, preferred_element_type=jnp.float32)
+        crossed = jnp.einsum(
+            "rkp,ikp->ri", block, filtered[:, :, cut], preferred_element_type=jnp.float32
+        )
+        quadratic = jnp.einsum(
+            "rp,ip->ri", power, envelope[:, cut], preferred_element_type=jnp.float32
+        )
         return crossed - quadratic
 
     parts = []
-    for block in (references, first, second):
-        mine = partial(block)
+    for pieces in ([(references, slice(None))], [(first, slice(None))], list(zip(second, columns))):
+        mine = sum(partial(block, cut) for block, cut in pieces)
         parts.append(mine + passed_along(mine, "shell", 1))
     scores = jnp.concatenate(parts, 0)
     live_slots = jnp.arange(capacity, dtype=jnp.int32) < live_count[0]
@@ -72,17 +79,17 @@
         jnp.bfloat16
     )
     here, back_1, back_2 = [posterior[s * per_block : (s + 1) * per_block] for s in range(3)]
-    width = pixels // CHUNKS
-    columns = [slice(c * width, (c + 1) * width) for c in range(CHUNKS)]
 
     def sums(rows, cut):
         return jnp.einsum(
             "ri,ikp->rkp", rows, filtered[:, :, cut], preferred_element_type=jnp.float32
         )
 
-    returned_1 = passed_along(back_1, "blk", -1)
-    returned_2 = passed_along(back_2, "blk", -2)
-    farther = [passed_along(sums(back_2, cut).astype(jnp.bfloat16), "blk", -1) for cut in columns]
+    leaving = [sums(back_2, cut).astype(jnp.bfloat16) for cut in columns]
+    farther = [passed_along(value, "blk", -1) for value in leaving]
+    sent_1, sent_2, _ = lax.optimization_barrier((back_1, back_2, leaving[-1]))
+    returned_1 = passed_along(sent_1, "blk", -1)
+    returned_2 = passed_along(sent_2, "blk", -2)
     nearer = [
         passed_along((sums(back_1, cut) + got.astype(jnp.float32)).astype(jnp.bfloat16), "blk", -1)
         for cut, got in zip(columns, farther)

time: 93 us -> 96.7 us (1.040)
  waiting for transfers between devices: 17.9 us -> 26.2 us
  starting transfers between devices: 20.7 us -> 14.3 us
  other arithmetic: 18.4 us -> 19.6 us
    ppermute x13 -> x14, waiting for transfers between devices: 17.9 us -> 26.2 us  [passed_along(): return lax.ppermute(value, axis, pairs)]
    convert_element_type x1 -> x0, other arithmetic: 6.93 us -> none  [body(): envelope = (contrast * contrast * half_weight).astype(jnp.bfloat16)]
    mul x1 -> x2, other arithmetic: 0.73 us -> 7.65 us  [the longest x1 6.92 us: body(): contrast * weight]
    ppermute x13 -> x14, starting transfers between devices: 20.7 us -> 14.3 us  [passed_along(): return lax.ppermute(value, axis, pairs)]
    convert_element_type x3 -> x4, other arithmetic: 2.51 us -> 3.66 us  [partial(): wide = block.astype(jnp.float32)]
    dot_general x6 -> x8, matrix products: 12.3 us -> 12.5 us  [the longest x4 8.13 us: partial(): jnp.einsum('rkp,ikp->ri', block, filtered[:, :, cut], preferred_element_t...]
  transfers between devices with their start and end apart: 13 -> 14, of which waited for: 5 -> 8; matrix products, arithmetic and copies ran while one was open for 50% -> 52% of each run, Pallas kernels for 0% -> 0%
where the time goes in v2:
time: 96.7 us; the launch traced here: 96.3 us
  matrix products  31.7 us (33%)
  waiting for transfers between devices  26.2 us (27%)
  other arithmetic  19.6 us (20%)
  starting transfers between devices  14.3 us (15%)
  local copies, waits for them, and re-layouts  3.08 us (3%)
  between operations  1.58 us (2%)
    ppermute x14, waiting for transfers between devices, passed_along(): return lax.ppermute(value, axis, pairs)  26.2 us
    ppermute x14, starting transfers between devices, passed_along(): return lax.ppermute(value, axis, pairs)  14.3 us
    dot_general x3, matrix products, body(): jnp.einsum('ri,ip->rp', rows, values, preferred_element_type=jnp.float32)  13.7 us
    dot_general x4, matrix products, partial(): jnp.einsum('rkp,ikp->ri', block, filtered[:, :, cut], preferred_element_t...  8.13 us
    mul x1, other arithmetic, body(): contrast * weight  6.92 us
    convert_element_type x1, other arithmetic, body(): (images.astype(jnp.float32) * (contrast * weight)[:, None, :]).astype(jnp...  6.88 us
    dot_general x6, matrix products, sums(): jnp.einsum('ri,ikp->rkp', rows, filtered[:, :, cut], preferred_element_ty...  5.52 us
    dot_general x4, matrix products, partial(): jnp.einsum('rp,ip->ri', power, envelope[:, cut], preferred_element_type=j...  4.33 us
  transfers between devices with their start and end apart: 14, of which 8 were waited for; matrix products, arithmetic and copies ran while one was open for 52% of the time, Pallas kernels for 0%

profile of v2, /device:TPU:0, one launch (start us, length us, event | category | flops | bytes accessed | tf_op | source)
XLA Modules:
  0.0 96.3 jit_solution(17594255862176559846)
XLA Ops:
  0.6 0.0 slice-start
  0.6 5.5 %collective-permute-start.11 = (f32[512]{0:T(512)}, f32[512]{0:T(512)S(1)}, u32[]{:S(2)}, u32[]{:S(2)}) collective-permute-start(f32[512]{0:T(512)} %param.9), channel_id=1, source_target_pairs={{0,30},{2,0},{4,2},{6,4},{8,6},{10,8},{12,10},{14,12},{16,14},{18,... | collective-permute-start | bytes 6152 | tf_op jit(solution)/shard_map/ppermute | solution.py:15
  6.1 0.6 collective-permute-start.13
  6.8 3.3 %copy_convert_fusion = (f32[64,2,4096]{2,0,1:T(8,128)}, bf16[64,2,4096]{2,0,1:T(8,128)(2,1)S(1)}) fusion(bf16[64,2,4096]{2,1,0:T(2,128)(2,1)} %param.8), kind=kLoop, calls=%fused_computation.137 | loop fusion | flops 524288 | bytes 4194304 | tf_op jit(solution)/shard_map/convert_element_type | solution.py:59
  10.0 0.2 collective-permute-start
  10.2 1.0 %select_reduce_fusion = f32[4096]{0:T(1024)S(1)} fusion(f32[64]{0:T(128)} %param.12, s32[4096]{0:T(1024)} %param.11), kind=kLoop, calls=%fused_computation.83 | loop fusion | flops 782336 | bytes 33024 | tf_op jit(solution)/shard_map/reduce_sum | solution.py:42
  11.2 0.7 broadcast_multiply_fusion.2
  12.6 0.0 slice-start.1
  12.6 6.9 %broadcast_multiply_fusion = (f32[512,4096]{1,0:T(8,128)S(1)}, bf16[512,4096]{1,0:T(8,128)(2,1)S(1)}) fusion(f32[4096]{0:T(1024)S(1)} %get-tuple-element.36, f32[4096]{0:T(1024)S(1)} %broadcast_multiply_fusion.2, f32[512]{0:T(512)} %param.9, f32[4096]{0:T(1024)S(1)} %get-tuple-element.37), kind=kLoop, calls=%fused_computation.34 | loop fusion | flops 46137344 | bytes 12634112 | tf_op jit(solution)/shard_map/mul | solution.py:53
  19.5 0.0 slice-done
  19.5 0.0 slice-done.1
  19.5 6.9 %multiply_convert_fusion = bf16[512,2,4096]{2,0,1:T(8,128)(2,1)S(1)} fusion(bf16[512,2,4096]{2,1,0:T(2,128)(2,1)S(1)} %bitcast.61, f32[512,4096]{1,0:T(8,128)S(1)} %get-tuple-element.34), kind=kLoop, calls=%fused_computation | loop fusion | flops 12582912 | bytes 25165824 | tf_op jit(solution)/shard_map/convert_element_type | solution.py:53
  26.4 0.5 collective-permute-done
  27.0 0.2 convert_element_type.84
  27.2 0.0 copy-start
  27.2 0.1 fusion.130
  27.3 1.4 %fusion.87 = f32[64,512]{1,0:T(8,128)S(1)} fusion(bf16[512,4096]{1,0:T(8,128)(2,1)S(1)} %get-tuple-element.9, f32[64,2,4096]{2,0,1:T(8,128)S(1)} %convert_element_type.84), kind=kOutput, calls=%fused_computation.88 | convolution fusion | flops 269484032 | bytes 6422528 | tf_op jit(solution)/shard_map/rp,ip->ri/dot_general | solution.py:64
  28.7 2.7 %fusion.68 = f32[64,512]{1,0:T(8,128)S(1)} fusion(f32[64,512]{1,0:T(8,128)S(1)} %fusion.87, bf16[64,2,4096]{2,0,1:T(8,128)(2,1)S(1)} %collective-permute-done, bf16[512,2,4096]{2,0,1:T(8,128)(2,1)S(1)} %multiply_convert_fusion), kind=kOutput, calls=%fused_computation.69 | convolution fusion | flops 536903680 | bytes 9699328 | tf_op jit(solution)/shard_map/rkp,ikp->ri/dot_general | solution.py:61
  31.4 1.5 %collective-permute-start.2 = (f32[64,512]{1,0:T(8,128)S(1)}, f32[64,512]{1,0:T(8,128)S(1)}, u32[]{:S(2)}, u32[]{:S(2)}) collective-permute-start(f32[64,512]{1,0:T(8,128)S(1)} %fusion.68), channel_id=1, source_target_pairs={{0,1},{1,0},{2,3},{3,2},{4,5},{5,4},{6,7},{7,6},{8,9},{9,8},{10,11... | collective-permute-start | bytes 393224 | tf_op jit(solution)/shard_map/ppermute | solution.py:15
  32.9 0.6 collective-permute-start.4
  33.5 0.3 collective-permute-start.3
  33.8 1.4 %fusion.84 = f32[64,512]{1,0:T(8,128)S(1)} fusion(bf16[512,4096]{1,0:T(8,128)(2,1)S(1)} %get-tuple-element.9, f32[64,2,4096]{2,0,1:T(8,128)S(1)} %copy-done), kind=kOutput, calls=%fused_computation.86 | convolution fusion | flops 269484032 | bytes 6422528 | tf_op jit(solution)/shard_map/rp,ip->ri/dot_general | solution.py:64
  35.1 0.0 copy-done.1
  35.2 2.7 %fusion.69 = f32[64,512]{1,0:T(8,128)S(1)} fusion(f32[64,512]{1,0:T(8,128)S(1)} %fusion.84, bf16[512,2,4096]{2,0,1:T(8,128)(2,1)S(1)} %multiply_convert_fusion, bf16[64,2,4096]{2,1,0:T(2,128)(2,1)S(1)} %copy-done.1), kind=kOutput, calls=%fused_computation.71 | convolution fusion | flops 536903680 | bytes 9699328 | tf_op jit(solution)/shard_map/rkp,ikp->ri/dot_general | solution.py:61
  37.8 0.0 collective-permute-done.2
  37.8 1.3 %collective-permute-start.1 = (f32[64,512]{1,0:T(8,128)S(1)}, f32[64,512]{1,0:T(8,128)S(1)}, u32[]{:S(2)}, u32[]{:S(2)}) collective-permute-start(f32[64,512]{1,0:T(8,128)S(1)} %fusion.69), channel_id=1, source_target_pairs={{0,1},{1,0},{2,3},{3,2},{4,5},{5,4},{6,7},{7,6},{8,9},{9,8},{10,11... | collective-permute-start | bytes 393224 | tf_op jit(solution)/shard_map/ppermute | solution.py:15
  39.2 5.0 %collective-permute-done.4 = bf16[64,2,2048]{2,0,1:T(8,128)(2,1)S(1)} collective-permute-done((bf16[64,2,2048]{2,0,1:T(8,128)(2,1)S(1)}, bf16[64,2,2048]{2,0,1:T(8,128)(2,1)S(1)}, u32[]{:S(2)}, u32[]{:S(2)}) %collective-permute-start.4) | collective-permute-done | bytes 524320 | tf_op jit(solution)/shard_map/ppermute | solution.py:15
  44.2 0.1 convert_element_type.90
  44.3 0.8 fusion.58
  45.1 4.7 %collective-permute-done.3 = bf16[64,2,2048]{2,0,1:T(8,128)(2,1)S(1)} collective-permute-done((bf16[64,2,2048]{2,0,1:T(8,128)(2,1)S(1)}, bf16[64,2,2048]{2,0,1:T(8,128)(2,1)S(1)}, u32[]{:S(2)}, u32[]{:S(2)}) %collective-permute-start.3) | collective-permute-done | bytes 524320 | tf_op jit(solution)/shard_map/ppermute | solution.py:15
  49.8 0.1 convert_element_type.87
  49.9 0.8 fusion.60
  50.7 1.4 %fusion.70 = f32[64,512]{1,0:T(8,128)S(1)} fusion(f32[64,512]{1,0:T(8,128)S(1)} %fusion.58, bf16[64,2,2048]{2,0,1:T(8,128)(2,1)S(1)} %collective-permute-done.4, bf16[512,2,4096]{2,0,1:T(8,128)(2,1)S(1)} %multiply_convert_fusion), kind=kOutput, calls=%fused_computation.72 | convolution fusion | flops 268468224 | bytes 4980736 | tf_op jit(solution)/shard_map/rkp,ikp->ri/dot_general | solution.py:61
  52.1 1.4 %fusion.76 = f32[64,512]{1,0:T(8,128)S(1)} fusion(f32[64,512]{1,0:T(8,128)S(1)} %fusion.70, f32[64,512]{1,0:T(8,128)S(1)} %fusion.60, bf16[64,2,2048]{2,0,1:T(8,128)(2,1)S(1)} %collective-permute-done.3, bf16[512,2,4096]{2,0,1:T(8,128)(2,1)S(1)} %multiply_convert_fusion), kind=kOutput, calls=%fused_computation.74 | convolution fusion | flops 268500992 | bytes 5111808 | tf_op jit(solution)/shard_map/rkp,ikp->ri/dot_general | solution.py:61
  53.5 0.6 collective-permute-start.5
  54.1 0.0 collective-permute-done.1
  54.1 4.4 %collective-permute-done.5 = f32[64,512]{1,0:T(8,128)S(1)} collective-permute-done((f32[64,512]{1,0:T(8,128)S(1)}, f32[64,512]{1,0:T(8,128)S(1)}, u32[]{:S(2)}, u32[]{:S(2)}) %collective-permute-start.5) | collective-permute-done | bytes 131104 | tf_op jit(solution)/shard_map/ppermute | solution.py:15
  58.6 0.1 exponential_reduce_fusion
  58.7 0.1 select_convert_fusion
  58.8 0.9 fusion.49
  59.7 0.1 collective-permute-start.10
  59.7 0.9 fusion.46
  60.6 0.1 collective-permute-start.8
  60.7 0.1 collective-permute-start.12
  60.7 0.0 collective-permute-done.11
  60.7 0.3 collective-permute-start.6
  61.0 0.6 collective-permute-done.10
  61.6 5.9 %fusion.16 = f32[64,4096]{1,0:T(8,128)S(1)} fusion(bf16[64,512]{1,0:T(8,128)(2,1)S(1)} %collective-permute-done.10, f32[512]{0:T(512)S(1)} %collective-permute-done.11, f32[4096]{0:T(1024)S(1)} %get-tuple-element.37, f32[4096]{0:T(1024)S(1)} %broadcast_multiply_fusion.2), kind=kOutput, calls=%fused_computation.35 | convolution fusion | flops 312475648 | bytes 1148928 | tf_op jit(solution)/shard_map/ri,ip->rp/dot_general | solution.py:101
  67.5 0.0 collective-permute-done.13
  67.5 3.3 %collective-permute-done.12 = bf16[64,512]{1,0:T(8,128)(2,1)S(1)} collective-permute-done((bf16[64,512]{1,0:T(8,128)(2,1)S(1)}, bf16[64,512]{1,0:T(8,128)(2,1)S(1)}, u32[]{:S(2)}, u32[]{:S(2)}) %collective-permute-start.12) | collective-permute-done | bytes 65568 | tf_op jit(solution)/shard_map/ppermute | solution.py:15
  70.8 5.9 %fusion.17 = f32[64,4096]{1,0:T(8,128)S(1)} fusion(bf16[64,512]{1,0:T(8,128)(2,1)S(1)} %collective-permute-done.12, f32[512]{0:T(512)S(1)} %collective-permute-done.13, f32[4096]{0:T(1024)S(1)} %get-tuple-element.37, f32[4096]{0:T(1024)S(1)} %broadcast_multiply_fusion.2), kind=kOutput, calls=%fused_computation.36 | convolution fusion | flops 312475648 | bytes 1148928 | tf_op jit(solution)/shard_map/ri,ip->rp/dot_general | solution.py:101
  76.7 0.0 collective-permute-done.6
  76.7 1.1 %fusion.55 = bf16[64,2,2048]{2,0,1:T(8,128)(2,1)S(1)} fusion(bf16[512,2,4096]{2,0,1:T(8,128)(2,1)S(1)} %multiply_convert_fusion, bf16[64,2,2048]{2,0,1:T(8,128)(2,1)S(1)} %collective-permute-done.6, bf16[192,512]{1,0:T(8,128)(2,1)S(1)} %select_convert_fusion), kind=kOutput, calls=%fused_computation.60 | convolution fusion | flops 269221888 | bytes 5308416 | tf_op jit(solution)/shard_map/ri,ikp->rkp/dot_general | solution.py:84
  77.9 2.2 %collective-permute-start.7 = (bf16[64,2,2048]{2,0,1:T(8,128)(2,1)S(1)}, bf16[64,2,2048]{2,0,1:T(8,128)(2,1)S(1)}, u32[]{:S(2)}, u32[]{:S(2)}) collective-permute-start(bf16[64,2,2048]{2,0,1:T(8,128)(2,1)S(1)} %fusion.55), channel_id=1, source_target_pairs={{0,30},{2,0},{4,2},{6,4},{8,6},{10,8},{12,10},{14,12},{16,14},{18,... | collective-permute-start | bytes 1572872 | tf_op jit(solution)/shard_map/ppermute | solution.py:15
  80.1 0.0 collective-permute-done.8
  80.1 0.9 fusion.52
  80.9 1.0 %collective-permute-start.9 = (bf16[64,2,2048]{2,0,1:T(8,128)(2,1)S(1)}, bf16[64,2,2048]{2,0,1:T(8,128)(2,1)S(1)}, u32[]{:S(2)}, u32[]{:S(2)}) collective-permute-start(bf16[64,2,2048]{2,0,1:T(8,128)(2,1)S(1)} %fusion.52), channel_id=1, source_target_pairs={{0,30},{2,0},{4,2},{6,4},{8,6},{10,8},{12,10},{14,12},{16,14},{18,... | collective-permute-start | bytes 1572872 | tf_op jit(solution)/shard_map/ppermute | solution.py:15
  82.0 1.9 %fusion.15 = f32[64,4096]{1,0:T(8,128)} fusion(f32[64,4096]{1,0:T(8,128)S(1)} %fusion.17, f32[64,4096]{1,0:T(8,128)S(1)} %fusion.16, bf16[512,4096]{1,0:T(8,128)(2,1)S(1)} %get-tuple-element.9, bf16[192,512]{1,0:T(8,128)(2,1)S(1)} %select_convert_fusion), kind=kOutput, calls=%fused_computation.33 | convolution fusion | flops 268959744 | bytes 7405568 | tf_op jit(solution)/shard_map/ri,ip->rp/dot_general | solution.py:101
  83.9 2.9 %collective-permute-done.7 = bf16[64,2,2048]{2,0,1:T(8,128)(2,1)S(1)} collective-permute-done((bf16[64,2,2048]{2,0,1:T(8,128)(2,1)S(1)}, bf16[64,2,2048]{2,0,1:T(8,128)(2,1)S(1)}, u32[]{:S(2)}, u32[]{:S(2)}) %collective-permute-start.7) | collective-permute-done | bytes 524320 | tf_op jit(solution)/shard_map/ppermute | solution.py:15
  86.8 0.9 fusion.34
  87.6 4.7 %collective-permute-done.9 = bf16[64,2,2048]{2,0,1:T(8,128)(2,1)S(1)} collective-permute-done((bf16[64,2,2048]{2,0,1:T(8,128)(2,1)S(1)}, bf16[64,2,2048]{2,0,1:T(8,128)(2,1)S(1)}, u32[]{:S(2)}, u32[]{:S(2)}) %collective-permute-start.9) | collective-permute-done | bytes 524320 | tf_op jit(solution)/shard_map/ppermute | solution.py:15
  92.4 0.9 fusion.40
  93.3 0.1 pad_maximum_fusion
  93.4 2.9 %copy.23 = f32[64,2,4096]{2,1,0:T(2,128)} copy(f32[64,2,4096]{2,0,1:T(8,128)S(1)} %pad_maximum_fusion) | data formatting | bytes 4194304
  (13 shorter events, 0.2 us)
Async XLA Ops:
  0.6 18.9 %slice-start = ((s8[8388608]{0:T(1024)(128)(4,1)}), s8[4194304]{0:T(1024)(128)(4,1)S(1)}, s32[]{:S(2)}) async-start(s8[8388608]{0:T(1024)(128)(4,1)} %bitcast.60), calls=%async_computation | async-start | bytes 8388608
  0.6 60.1 %collective-permute-start.11 = (f32[512]{0:T(512)}, f32[512]{0:T(512)S(1)}, u32[]{:S(2)}, u32[]{:S(2)}) collective-permute-start(f32[512]{0:T(512)} %param.9), channel_id=1, source_target_pairs={{0,30},{2,0},{4,2},{6,4},{8,6},{10,8},{12,10},{14,12},{16,14},{18,... | collective-permute-start | bytes 6152 | tf_op jit(solution)/shard_map/ppermute | solution.py:15
  6.1 61.4 %collective-permute-start.13 = (f32[512]{0:T(512)}, f32[512]{0:T(512)S(1)}, u32[]{:S(2)}, u32[]{:S(2)}) collective-permute-start(f32[512]{0:T(512)} %param.9), channel_id=1, source_target_pairs={{0,28},{2,30},{4,0},{6,2},{8,4},{10,6},{12,8},{14,10},{16,12},{18,... | collective-permute-start | bytes 6152 | tf_op jit(solution)/shard_map/ppermute | solution.py:15
  10.0 16.9 %collective-permute-start = (bf16[64,2,4096]{2,0,1:T(8,128)(2,1)S(1)}, bf16[64,2,4096]{2,0,1:T(8,128)(2,1)S(1)}, u32[]{:S(2)}, u32[]{:S(2)}) collective-permute-start(bf16[64,2,4096]{2,0,1:T(8,128)(2,1)S(1)} %get-tuple-element.29), channel_id=1, source_target_pairs={{0,2},{2,4},{4,6},{6,8},{8,10},{10,12},{12,14},{14,16},{16,18},{18... | collective-permute-start | bytes 3145736 | tf_op jit(solution)/shard_map/ppermute | solution.py:15
  12.6 7.0 %slice-start.1 = ((s8[8388608]{0:T(1024)(128)(4,1)}), s8[4194304]{0:T(1024)(128)(4,1)S(1)}, s32[]{:S(2)}) async-start(s8[8388608]{0:T(1024)(128)(4,1)} %bitcast.60), calls=%async_computation.1 | async-start | bytes 8388608
  27.2 6.6 %copy-start = (f32[64,2,4096]{2,0,1:T(8,128)S(1)}, f32[64,2,4096]{2,0,1:T(8,128)}, u32[]{:S(2)}) copy-start(f32[64,2,4096]{2,0,1:T(8,128)} %get-tuple-element.28) | copy-start | bytes 6291460
  28.7 6.5 %copy-start.1 = (bf16[64,2,4096]{2,1,0:T(2,128)(2,1)S(1)}, bf16[64,2,4096]{2,1,0:T(2,128)(2,1)}, u32[]{:S(2)}) copy-start(bf16[64,2,4096]{2,1,0:T(2,128)(2,1)} %param.8) | copy-start | bytes 3145732
  31.4 6.5 %collective-permute-start.2 = (f32[64,512]{1,0:T(8,128)S(1)}, f32[64,512]{1,0:T(8,128)S(1)}, u32[]{:S(2)}, u32[]{:S(2)}) collective-permute-start(f32[64,512]{1,0:T(8,128)S(1)} %fusion.68), channel_id=1, source_target_pairs={{0,1},{1,0},{2,3},{3,2},{4,5},{5,4},{6,7},{7,6},{8,9},{9,8},{10,11... | collective-permute-start | bytes 393224 | tf_op jit(solution)/shard_map/ppermute | solution.py:15
  32.9 11.3 %collective-permute-start.4 = (bf16[64,2,2048]{2,0,1:T(8,128)(2,1)S(1)}, bf16[64,2,2048]{2,0,1:T(8,128)(2,1)S(1)}, u32[]{:S(2)}, u32[]{:S(2)}) collective-permute-start(bf16[64,2,2048]{2,0,1:T(8,128)(2,1)S(1)} %get-tuple-element.31), channel_id=1, source_target_pairs={{0,2},{2,4},{4,6},{6,8},{8,10},{10,12},{12,14},{14,16},{16,18},{18... | collective-permute-start | bytes 1572872 | tf_op jit(solution)/shard_map/ppermute | solution.py:15
  33.5 16.4 %collective-permute-start.3 = (bf16[64,2,2048]{2,0,1:T(8,128)(2,1)S(1)}, bf16[64,2,2048]{2,0,1:T(8,128)(2,1)S(1)}, u32[]{:S(2)}, u32[]{:S(2)}) collective-permute-start(bf16[64,2,2048]{2,0,1:T(8,128)(2,1)S(1)} %get-tuple-element.30), channel_id=1, source_target_pairs={{0,2},{2,4},{4,6},{6,8},{8,10},{10,12},{12,14},{14,16},{16,18},{18... | collective-permute-start | bytes 1572872 | tf_op jit(solution)/shard_map/ppermute | solution.py:15
  37.8 16.3 %collective-permute-start.1 = (f32[64,512]{1,0:T(8,128)S(1)}, f32[64,512]{1,0:T(8,128)S(1)}, u32[]{:S(2)}, u32[]{:S(2)}) collective-permute-start(f32[64,512]{1,0:T(8,128)S(1)} %fusion.69), channel_id=1, source_target_pairs={{0,1},{1,0},{2,3},{3,2},{4,5},{5,4},{6,7},{7,6},{8,9},{9,8},{10,11... | collective-permute-start | bytes 393224 | tf_op jit(solution)/shard_map/ppermute | solution.py:15
  53.5 5.0 %collective-permute-start.5 = (f32[64,512]{1,0:T(8,128)S(1)}, f32[64,512]{1,0:T(8,128)S(1)}, u32[]{:S(2)}, u32[]{:S(2)}) collective-permute-start(f32[64,512]{1,0:T(8,128)S(1)} %fusion.76), channel_id=1, source_target_pairs={{0,1},{1,0},{2,3},{3,2},{4,5},{5,4},{6,7},{7,6},{8,9},{9,8},{10,11... | collective-permute-start | bytes 393224 | tf_op jit(solution)/shard_map/ppermute | solution.py:15
  58.7 8.8 %copy-start.2 = (f32[512]{0:T(512)}, f32[512]{0:T(512)S(1)}, u32[]{:S(2)}) copy-start(f32[512]{0:T(512)S(1)} %add_select_fusion) | copy-start | bytes 6148
  59.7 2.0 %collective-permute-start.10 = (bf16[64,512]{1,0:T(8,128)(2,1)S(1)}, bf16[64,512]{1,0:T(8,128)(2,1)S(1)}, u32[]{:S(2)}, u32[]{:S(2)}) collective-permute-start(bf16[64,512]{1,0:T(8,128)(2,1)S(1)} %get-tuple-element.11), channel_id=1, source_target_pairs={{0,30},{2,0},{4,2},{6,4},{8,6},{10,8},{12,10},{14,12},{16,14},{18,... | collective-permute-start | bytes 196616 | tf_op jit(solution)/shard_map/ppermute | solution.py:15
  60.6 19.5 %collective-permute-start.8 = (bf16[64,2,2048]{2,0,1:T(8,128)(2,1)S(1)}, bf16[64,2,2048]{2,0,1:T(8,128)(2,1)S(1)}, u32[]{:S(2)}, u32[]{:S(2)}) collective-permute-start(bf16[64,2,2048]{2,0,1:T(8,128)(2,1)S(1)} %fusion.49), channel_id=1, source_target_pairs={{0,30},{2,0},{4,2},{6,4},{8,6},{10,8},{12,10},{14,12},{16,14},{18,... | collective-permute-start | bytes 1572872 | tf_op jit(solution)/shard_map/ppermute | solution.py:15
  60.7 10.2 %collective-permute-start.12 = (bf16[64,512]{1,0:T(8,128)(2,1)S(1)}, bf16[64,512]{1,0:T(8,128)(2,1)S(1)}, u32[]{:S(2)}, u32[]{:S(2)}) collective-permute-start(bf16[64,512]{1,0:T(8,128)(2,1)S(1)} %get-tuple-element.12), channel_id=1, source_target_pairs={{0,28},{2,30},{4,0},{6,2},{8,4},{10,6},{12,8},{14,10},{16,12},{18,... | collective-permute-start | bytes 196616 | tf_op jit(solution)/shard_map/ppermute | solution.py:15
  60.7 16.0 %collective-permute-start.6 = (bf16[64,2,2048]{2,0,1:T(8,128)(2,1)S(1)}, bf16[64,2,2048]{2,0,1:T(8,128)(2,1)S(1)}, u32[]{:S(2)}, u32[]{:S(2)}) collective-permute-start(bf16[64,2,2048]{2,0,1:T(8,128)(2,1)S(1)} %fusion.46), channel_id=1, source_target_pairs={{0,30},{2,0},{4,2},{6,4},{8,6},{10,8},{12,10},{14,12},{16,14},{18,... | collective-permute-start | bytes 1572872 | tf_op jit(solution)/shard_map/ppermute | solution.py:15
  77.9 8.9 %collective-permute-start.7 = (bf16[64,2,2048]{2,0,1:T(8,128)(2,1)S(1)}, bf16[64,2,2048]{2,0,1:T(8,128)(2,1)S(1)}, u32[]{:S(2)}, u32[]{:S(2)}) collective-permute-start(bf16[64,2,2048]{2,0,1:T(8,128)(2,1)S(1)} %fusion.55), channel_id=1, source_target_pairs={{0,30},{2,0},{4,2},{6,4},{8,6},{10,8},{12,10},{14,12},{16,14},{18,... | collective-permute-start | bytes 1572872 | tf_op jit(solution)/shard_map/ppermute | solution.py:15
  80.9 11.4 %collective-permute-start.9 = (bf16[64,2,2048]{2,0,1:T(8,128)(2,1)S(1)}, bf16[64,2,2048]{2,0,1:T(8,128)(2,1)S(1)}, u32[]{:S(2)}, u32[]{:S(2)}) collective-permute-start(bf16[64,2,2048]{2,0,1:T(8,128)(2,1)S(1)} %fusion.52), channel_id=1, source_target_pairs={{0,30},{2,0},{4,2},{6,4},{8,6},{10,8},{12,10},{14,12},{16,14},{18,... | collective-permute-start | bytes 1572872 | tf_op jit(solution)/shard_map/ppermute | solution.py:15

commit v3 on v1

--- a/solution.py
+++ b/solution.py
@@ -12,6 +12,12 @@
 def passed_along(value, axis, steps):
     count = lax.axis_size(axis)
     pairs = [(source, (source + steps) % count) for source in range(count)]
+    return lax.ppermute(value, axis, pairs)
+
+
+def passed_by_even(value, axis, steps):
+    count = lax.axis_size(axis)
+    pairs = [(source, (source + steps) % count) for source in range(0, count, 2)]
     return lax.ppermute(value, axis, pairs)
 
 
@@ -32,9 +38,7 @@
     per_block, _, pixels = references.shape
     shells = noise_power.shape[0]
     first = passed_along(references, "blk", 1)
-    second = passed_along(first, "blk", 1)
-    defocus_1 = passed_along(defocus, "blk", -1)
-    defocus_2 = passed_along(defocus, "blk", -2)
+    direct = passed_by_even(references, "blk", 2)
     lookup = jnp.where(
         jnp.arange(shells, dtype=jnp.int32)[:, None] == shell_index[None, :],
         noise_power[:, None],
@@ -59,8 +63,18 @@
         quadratic = jnp.einsum("rp,ip->ri", power, envelope, preferred_element_type=jnp.float32)
         return crossed - quadratic
 
-    parts = []
-    for block in (references, first, second):
+    mine = partial(references)
+    mine, defocus_sent = lax.optimization_barrier((mine, defocus))
+    defocus_1 = passed_along(defocus_sent, "blk", -1)
+    defocus_2 = passed_along(defocus_sent, "blk", -2)
+    mine, first, direct, defocus_1, defocus_2 = lax.optimization_barrier(
+        (mine, first, direct, defocus_1, defocus_2)
+    )
+    paired = passed_by_even(first, "blk", 1)
+    parts = [mine + passed_along(mine, "shell", 1)]
+    even = lax.rem(lax.axis_index("blk"), 2) == 0
+    second = jnp.where(even, direct, paired)
+    for block in (first, second):
         mine = partial(block)
         parts.append(mine + passed_along(mine, "shell", 1))
     scores = jnp.concatenate(parts, 0)
@@ -83,10 +97,12 @@
     returned_1 = passed_along(back_1, "blk", -1)
     returned_2 = passed_along(back_2, "blk", -2)
     farther = [passed_along(sums(back_2, cut).astype(jnp.bfloat16), "blk", -1) for cut in columns]
-    nearer = [
-        passed_along((sums(back_1, cut) + got.astype(jnp.float32)).astype(jnp.bfloat16), "blk", -1)
+    joined = [
+        (sums(back_1, cut) + got.astype(jnp.float32)).astype(jnp.bfloat16)
         for cut, got in zip(columns, farther)
     ]
+    nearer = [passed_along(value, "blk", -1) for value in joined]
+    defocus_2, _ = lax.optimization_barrier((defocus_2, joined[-1]))
     numerator = jnp.concatenate(
         [sums(here, cut) + got.astype(jnp.float32) for cut, got in zip(columns, nearer)], 2
     )

time: 93 us -> 94.1 us (1.012)
  waiting for transfers between devices: 17.9 us -> 5.08 us
  starting transfers between devices: 20.7 us -> 29.4 us
  local copies, waits for them, and re-layouts: 2.98 us -> 6.2 us
  matrix products: 31 us -> 33.1 us
    ppermute x13 -> x12, waiting for transfers between devices: 17.9 us -> 5.07 us  [passed_along(): return lax.ppermute(value, axis, pairs)]
    ppermute x0 -> x2, starting transfers between devices: none -> 6.24 us  [passed_by_even(): return lax.ppermute(value, axis, pairs)]
    unnamed x11 -> x19, local copies, waits for them, and re-layouts: 2.97 us -> 6.19 us
    ppermute x13 -> x12, starting transfers between devices: 20.7 us -> 23.1 us  [passed_along(): return lax.ppermute(value, axis, pairs)]
    dot_general x3, matrix products: 4.24 us -> 6.41 us  [partial(): jnp.einsum('rp,ip->ri', power, envelope, preferred_element_type=jnp.float32)]
    convert_element_type x3 -> x2, other arithmetic: 2.51 us -> 0.35 us  [partial(): wide = block.astype(jnp.float32)]
    unnamed x1 -> x2, other arithmetic: 0.01 us -> 2.1 us
  transfers between devices with their start and end apart: 13 -> 14, of which waited for: 5 -> 4; matrix products, arithmetic and copies ran while one was open for 50% -> 49% of each run, Pallas kernels for 0% -> 0%
where the time goes in v3:
time: 94.1 us; the launch traced here: 93.7 us
  matrix products  33.1 us (35%)
  starting transfers between devices  29.4 us (31%)
  other arithmetic  18.4 us (20%)
  local copies, waits for them, and re-layouts  6.2 us (7%)
  waiting for transfers between devices  5.08 us (5%)
  between operations  1.6 us (2%)
    ppermute x12, starting transfers between devices, passed_along(): return lax.ppermute(value, axis, pairs)  23.1 us
    dot_general x3, matrix products, body(): jnp.einsum('ri,ip->rp', rows, values, preferred_element_type=jnp.float32)  13.7 us
    dot_general x3, matrix products, partial(): jnp.einsum('rkp,ikp->ri', block, filtered, preferred_element_type=jnp.flo...  7.98 us
    convert_element_type x1, other arithmetic, body(): envelope = (contrast * contrast * half_weight).astype(jnp.bfloat16)  6.93 us
    convert_element_type x1, other arithmetic, body(): (images.astype(jnp.float32) * (contrast * weight)[:, None, :]).astype(jnp...  6.89 us
    dot_general x3, matrix products, partial(): jnp.einsum('rp,ip->ri', power, envelope, preferred_element_type=jnp.float32)  6.41 us
    ppermute x2, starting transfers between devices, passed_by_even(): return lax.ppermute(value, axis, pairs)  6.24 us
    unnamed x19, local copies, waits for them, and re-layouts  6.19 us
  transfers between devices with their start and end apart: 14, of which 4 were waited for; matrix products, arithmetic and copies ran while one was open for 49% of the time, Pallas kernels for 0%

profile of v3, /device:TPU:0, one launch (start us, length us, event | category | flops | bytes accessed | tf_op | source)
XLA Modules:
  0.0 93.7 jit_solution(6329808032122015940)
XLA Ops:
  0.6 0.0 slice-start
  0.6 2.1 %fusion.120 = (bf16[64,2,4096]{2,0,1:T(8,128)(2,1)S(1)}, f32[64,2,4096]{2,0,1:T(8,128)S(1)}) fusion(bf16[64,2,4096]{2,1,0:T(2,128)(2,1)} %param.8), kind=kLoop, calls=%fused_computation.145 | loop fusion | flops 524288 | bytes 4194304 | tf_op args[1]
  2.7 0.5 collective-permute-start
  3.3 4.4 %collective-permute-start.1 = (bf16[64,2,4096]{2,0,1:T(8,128)(2,1)S(1)}, bf16[64,2,4096]{2,0,1:T(8,128)(2,1)S(1)}, u32[]{:S(2)}, u32[]{:S(2)}) collective-permute-start(bf16[64,2,4096]{2,0,1:T(8,128)(2,1)S(1)} %get-tuple-element.38), channel_id=1, source_target_pairs={{0,4},{4,8},{8,12},{12,16},{16,20},{20,24},{24,28},{28,0},{1,5},{5... | collective-permute-start | bytes 3145736 | tf_op jit(solution)/shard_map/ppermute | solution.py:21
  7.7 1.0 %select_reduce_fusion = f32[4096]{0:T(1024)S(1)} fusion(f32[64]{0:T(128)} %param.12, s32[4096]{0:T(1024)} %param.11), kind=kLoop, calls=%fused_computation.92 | loop fusion | flops 782336 | bytes 33024 | tf_op jit(solution)/shard_map/reduce_sum | solution.py:47
  8.7 0.7 broadcast_multiply_fusion.1
  9.4 6.9 %multiply_convert_fusion.3 = (bf16[512,4096]{1,0:T(8,128)(2,1)S(1)}, f32[512,4096]{1,0:T(8,128)S(1)}) fusion(f32[4096]{0:T(1024)S(1)} %get-tuple-element.44, f32[4096]{0:T(1024)S(1)} %get-tuple-element.46, f32[512]{0:T(512)} %param.9, f32[4096]{0:T(1024)S(1)} %get-tuple-element.45), kind=kLoop, calls=%fused_computation.24 | loop fusion | flops 46137344 | bytes 12634112 | tf_op jit(solution)/shard_map/convert_element_type | solution.py:52
  16.3 0.0 copy-start.2
  16.4 0.0 copy-start.4
  16.4 6.9 %multiply_convert_fusion = bf16[512,2,4096]{2,0,1:T(8,128)(2,1)S(1)} fusion(bf16[512,2,4096]{2,1,0:T(2,128)(2,1)S(1)} %bitcast.58, f32[512,4096]{1,0:T(8,128)S(1)} %get-tuple-element.43), kind=kLoop, calls=%fused_computation | loop fusion | flops 12582912 | bytes 25165824 | tf_op jit(solution)/shard_map/convert_element_type | solution.py:51
  23.3 0.0 copy-start.6
  23.3 3.2 %copy-done = bf16[512,2,4096]{2,0,1:T(8,128)(2,1)} copy-done((bf16[512,2,4096]{2,0,1:T(8,128)(2,1)}, bf16[512,2,4096]{2,0,1:T(8,128)(2,1)S(1)}, u32[]{:S(2)}) %copy-start) | copy-done | bytes 8388632
  26.5 2.7 %convolution_bitcast_fusion.2 = f32[64,512]{1,0:T(8,128)S(1)} fusion(bf16[512,2,4096]{2,0,1:T(8,128)(2,1)S(1)} %multiply_convert_fusion, bf16[64,2,4096]{2,1,0:T(2,128)(2,1)S(1)} %copy-done.4), kind=kOutput, calls=%fused_computation.75 | convolution fusion | flops 536870912 | bytes 9568256 | tf_op jit(solution)/shard_map/rkp,ikp->ri/dot_general | solution.py:62
  29.2 1.4 %convolution_subtract_fusion = f32[64,512]{1,0:T(8,128)S(1)} fusion(f32[64,512]{1,0:T(8,128)S(1)} %convolution_bitcast_fusion.2, bf16[512,4096]{1,0:T(8,128)(2,1)S(1)} %get-tuple-element.14, f32[64,2,4096]{2,0,1:T(8,128)S(1)} %get-tuple-element.39), kind=kOutput, calls=%fused_computation.70 | convolution fusion | flops 269516800 | bytes 6553600 | tf_op jit(solution)/shard_map/rp,ip->ri/dot_general | solution.py:63
  30.6 0.0 copy-done.6
  30.6 1.4 %collective-permute-start.2 = (f32[512]{0:T(512)S(1)}, f32[512]{0:T(512)S(1)}, u32[]{:S(2)}, u32[]{:S(2)}) collective-permute-start(f32[512]{0:T(512)S(1)} %copy-done.6), channel_id=1, source_target_pairs={{0,30},{2,0},{4,2},{6,4},{8,6},{10,8},{12,10},{14,12},{16,14},{18,... | collective-permute-start | bytes 6152 | tf_op jit(solution)/shard_map/ppermute | solution.py:15
  31.9 2.3 %collective-permute-start.3 = (f32[512]{0:T(512)S(1)}, f32[512]{0:T(512)S(1)}, u32[]{:S(2)}, u32[]{:S(2)}) collective-permute-start(f32[512]{0:T(512)S(1)} %copy-done.6), channel_id=1, source_target_pairs={{0,28},{2,30},{4,0},{6,2},{8,4},{10,6},{12,8},{14,10},{16,12},{18,... | collective-permute-start | bytes 6152 | tf_op jit(solution)/shard_map/ppermute | solution.py:15
  34.9 0.0 collective-permute-done.2
  34.9 0.6 collective-permute-done.3
  35.5 0.0 collective-permute-done
  35.5 0.0 collective-permute-done.1
  35.5 0.2 convert_element_type.75
  35.8 1.8 %collective-permute-start.6 = (bf16[64,2,4096]{2,0,1:T(8,128)(2,1)S(1)}, bf16[64,2,4096]{2,0,1:T(8,128)(2,1)S(1)}, u32[]{:S(2)}, u32[]{:S(2)}) collective-permute-start(bf16[64,2,4096]{2,0,1:T(8,128)(2,1)S(1)} %collective-permute-done), channel_id=1, source_target_pairs={{0,2},{4,6},{8,10},{12,14},{16,18},{20,22},{24,26},{28,30},{1,3},{... | collective-permute-start | bytes 3145736 | tf_op jit(solution)/shard_map/ppermute | solution.py:21
  37.6 2.0 %collective-permute-start.4 = (f32[64,512]{1,0:T(8,128)S(1)}, f32[64,512]{1,0:T(8,128)S(1)}, u32[]{:S(2)}, u32[]{:S(2)}) collective-permute-start(f32[64,512]{1,0:T(8,128)S(1)} %convolution_subtract_fusion), channel_id=1, source_target_pairs={{0,1},{1,0},{2,3},{3,2},{4,5},{5,4},{6,7},{7,6},{8,9},{9,8},{10,11... | collective-permute-start | bytes 393224 | tf_op jit(solution)/shard_map/ppermute | solution.py:15
  39.5 3.6 %fusion.64 = f32[64,512]{1,0:T(8,128)S(1)} fusion(bf16[512,4096]{1,0:T(8,128)(2,1)} %copy-done.2, f32[64,2,4096]{2,0,1:T(8,128)S(1)} %convert_element_type.75), kind=kOutput, calls=%fused_computation.97 | convolution fusion | flops 269484032 | bytes 6422528 | tf_op jit(solution)/shard_map/rp,ip->ri/dot_general | solution.py:63
  43.1 0.0 copy-done.1
  43.1 0.0 copy-start.3
  43.2 2.7 %fusion.54 = f32[64,512]{1,0:T(8,128)S(1)} fusion(f32[64,512]{1,0:T(8,128)S(1)} %fusion.64, bf16[64,2,4096]{2,0,1:T(8,128)(2,1)S(1)} %collective-permute-done, bf16[512,2,4096]{2,0,1:T(8,128)(2,1)S(1)} %copy-done.1), kind=kOutput, calls=%fused_computation.74 | convolution fusion | flops 536903680 | bytes 9699328 | tf_op jit(solution)/shard_map/rkp,ikp->ri/dot_general | solution.py:62
  45.8 0.2 collective-permute-start.5
  46.0 0.0 collective-permute-done.4
  46.0 0.0 collective-permute-done.6
  46.0 0.1 fusion.69
  46.2 0.0 copy-done.3
  46.2 1.4 %fusion.67 = f32[64,512]{1,0:T(8,128)S(1)} fusion(bf16[512,4096]{1,0:T(8,128)(2,1)S(1)} %copy-done.3, f32[64,2,4096]{2,0,1:T(8,128)S(1)} %fusion.69), kind=kOutput, calls=%fused_computation.99 | convolution fusion | flops 269484032 | bytes 6422528 | tf_op jit(solution)/shard_map/rp,ip->ri/dot_general | solution.py:63
  47.6 2.7 %fusion.53 = f32[64,512]{1,0:T(8,128)S(1)} fusion(f32[64,512]{1,0:T(8,128)S(1)} %fusion.67, bf16[512,2,4096]{2,0,1:T(8,128)(2,1)S(1)} %copy-done.1, bf16[64,2,4096]{2,0,1:T(8,128)(2,1)S(1)} %collective-permute-done.1, bf16[64,2,4096]{2,0,1:T(8,128)(2,1)S(1)} %collective-permute-done.6, pred[]{:T(512)S(6)} %eq.19), kind=kOutput, calls=%fused_computation.72 | convolution fusion | flops 537427968 | bytes 10747905 | tf_op jit(solution)/shard_map/rkp,ikp->ri/dot_general | solution.py:62
  50.3 2.0 %collective-permute-start.7 = (f32[64,512]{1,0:T(8,128)S(1)}, f32[64,512]{1,0:T(8,128)S(1)}, u32[]{:S(2)}, u32[]{:S(2)}) collective-permute-start(f32[64,512]{1,0:T(8,128)S(1)} %fusion.53), channel_id=1, source_target_pairs={{0,1},{1,0},{2,3},{3,2},{4,5},{5,4},{6,7},{7,6},{8,9},{9,8},{10,11... | collective-permute-start | bytes 393224 | tf_op jit(solution)/shard_map/ppermute | solution.py:15
  52.3 0.0 collective-permute-done.5
  52.3 3.0 %collective-permute-done.7 = f32[64,512]{1,0:T(8,128)S(1)} collective-permute-done((f32[64,512]{1,0:T(8,128)S(1)}, f32[64,512]{1,0:T(8,128)S(1)}, u32[]{:S(2)}, u32[]{:S(2)}) %collective-permute-start.7) | collective-permute-done | bytes 131104 | tf_op jit(solution)/shard_map/ppermute | solution.py:15
  55.4 0.1 exponential_reduce_fusion
  55.5 0.0 copy-start.5
  55.5 0.1 select_convert_fusion
  55.6 0.8 fusion.50
  56.4 0.8 fusion.93
  57.3 1.4 %collective-permute-start.12 = (bf16[64,512]{1,0:T(8,128)(2,1)S(1)}, bf16[64,512]{1,0:T(8,128)(2,1)S(1)}, u32[]{:S(2)}, u32[]{:S(2)}) collective-permute-start(bf16[64,512]{1,0:T(8,128)(2,1)S(1)} %get-tuple-element.41), channel_id=1, source_target_pairs={{0,30},{2,0},{4,2},{6,4},{8,6},{10,8},{12,10},{14,12},{16,14},{18,... | collective-permute-start | bytes 196616 | tf_op jit(solution)/shard_map/ppermute | solution.py:15
  58.7 0.8 fusion.47
  59.5 3.5 %collective-permute-start.10 = (bf16[64,2,2048]{2,0,1:T(8,128)(2,1)S(1)}, bf16[64,2,2048]{2,0,1:T(8,128)(2,1)S(1)}, u32[]{:S(2)}, u32[]{:S(2)}) collective-permute-start(bf16[64,2,2048]{2,0,1:T(8,128)(2,1)S(1)} %fusion.50), channel_id=1, source_target_pairs={{0,30},{2,0},{4,2},{6,4},{8,6},{10,8},{12,10},{14,12},{16,14},{18,... | collective-permute-start | bytes 1572872 | tf_op jit(solution)/shard_map/ppermute | solution.py:15
  63.1 0.0 collective-permute-start.13
  63.1 0.3 collective-permute-start.8
  63.4 0.0 collective-permute-done.12
  63.4 5.9 %convolution_add_fusion.1 = f32[64,4096]{1,0:T(8,128)S(1)} fusion(f32[64,4096]{1,0:T(8,128)S(1)} %fusion.93, bf16[64,512]{1,0:T(8,128)(2,1)S(1)} %collective-permute-done.12, f32[512]{0:T(512)S(1)} %collective-permute-done.2, f32[4096]{0:T(1024)S(1)} %get-tuple-element.44, f32[4096]{0:T(1024)S(1)} %get-tuple-element.46), kind=kOutput, calls=%fused_computation.33 | convolution fusion | flops 312737792 | bytes 2197504 | tf_op jit(solution)/shard_map/ri,ip->rp/dot_general | solution.py:110
  69.3 0.6 collective-permute-done.10
  69.9 0.8 add_convert_fusion
  70.8 4.7 %collective-permute-start.11 = (bf16[64,2,2048]{2,0,1:T(8,128)(2,1)S(1)}, bf16[64,2,2048]{2,0,1:T(8,128)(2,1)S(1)}, u32[]{:S(2)}, u32[]{:S(2)}) collective-permute-start(bf16[64,2,2048]{2,0,1:T(8,128)(2,1)S(1)} %add_convert_fusion), channel_id=1, source_target_pairs={{0,30},{2,0},{4,2},{6,4},{8,6},{10,8},{12,10},{14,12},{16,14},{18,... | collective-permute-start | bytes 1572872 | tf_op jit(solution)/shard_map/ppermute | solution.py:15
  75.5 0.8 collective-permute-done.8
  76.3 0.8 add_convert_fusion.1
  77.1 4.9 %collective-permute-start.9 = (bf16[64,2,2048]{2,0,1:T(8,128)(2,1)S(1)}, bf16[64,2,2048]{2,0,1:T(8,128)(2,1)S(1)}, u32[]{:S(2)}, u32[]{:S(2)}) collective-permute-start(bf16[64,2,2048]{2,0,1:T(8,128)(2,1)S(1)} %add_convert_fusion.1), channel_id=1, source_target_pairs={{0,30},{2,0},{4,2},{6,4},{8,6},{10,8},{12,10},{14,12},{16,14},{18,... | collective-permute-start | bytes 1572872 | tf_op jit(solution)/shard_map/ppermute | solution.py:15
  82.0 0.0 collective-permute-done.13
  82.0 6.9 %convolution_add_fusion = f32[64,4096]{1,0:T(8,128)} fusion(f32[64,4096]{1,0:T(8,128)S(1)} %convolution_add_fusion.1, bf16[64,512]{1,0:T(8,128)(2,1)S(1)} %collective-permute-done.13, f32[512]{0:T(512)S(1)} %collective-permute-done.3, f32[4096]{0:T(1024)S(1)} %get-tuple-element.44, f32[4096]{0:T(1024)S(1)} %get-tuple-element.46), kind=kOutput, calls=%fused_computation.32 | convolution fusion | flops 312737792 | bytes 2197504 | tf_op jit(solution)/shard_map/ri,ip->rp/dot_general | solution.py:110
  88.9 0.0 collective-permute-done.9
  88.9 0.8 convert_add_fusion.1
  89.8 0.0 collective-permute-done.11
  89.8 0.8 convert_add_fusion
  90.7 0.1 pad_maximum_fusion
  90.8 2.9 %copy.26 = f32[64,2,4096]{2,1,0:T(2,128)} copy(f32[64,2,4096]{2,0,1:T(8,128)S(1)} %pad_maximum_fusion) | data formatting | bytes 4194304
  (16 shorter events, 0.2 us)
Async XLA Ops:
  0.6 15.7 %slice-start = ((s8[8388608]{0:T(1024)(128)(4,1)}), s8[4194304]{0:T(1024)(128)(4,1)S(1)}, s32[]{:S(2)}) async-start(s8[8388608]{0:T(1024)(128)(4,1)} %bitcast.57), calls=%async_computation | async-start | bytes 8388608
  2.7 32.8 %collective-permute-start = (bf16[64,2,4096]{2,0,1:T(8,128)(2,1)S(1)}, bf16[64,2,4096]{2,0,1:T(8,128)(2,1)S(1)}, u32[]{:S(2)}, u32[]{:S(2)}) collective-permute-start(bf16[64,2,4096]{2,0,1:T(8,128)(2,1)S(1)} %get-tuple-element.38), channel_id=1, source_target_pairs={{0,2},{2,4},{4,6},{6,8},{8,10},{10,12},{12,14},{14,16},{16,18},{18... | collective-permute-start | bytes 3145736 | tf_op jit(solution)/shard_map/ppermute | solution.py:15
  3.3 32.3 %collective-permute-start.1 = (bf16[64,2,4096]{2,0,1:T(8,128)(2,1)S(1)}, bf16[64,2,4096]{2,0,1:T(8,128)(2,1)S(1)}, u32[]{:S(2)}, u32[]{:S(2)}) collective-permute-start(bf16[64,2,4096]{2,0,1:T(8,128)(2,1)S(1)} %get-tuple-element.38), channel_id=1, source_target_pairs={{0,4},{4,8},{8,12},{12,16},{16,20},{20,24},{24,28},{28,0},{1,5},{5... | collective-permute-start | bytes 3145736 | tf_op jit(solution)/shard_map/ppermute | solution.py:21
  9.4 7.0 %slice-start.1 = ((s8[8388608]{0:T(1024)(128)(4,1)}), s8[4194304]{0:T(1024)(128)(4,1)S(1)}, s32[]{:S(2)}) async-start(s8[8388608]{0:T(1024)(128)(4,1)} %bitcast.57), calls=%async_computation.1 | async-start | bytes 8388608
  16.3 12.8 %copy-start.2 = (bf16[512,4096]{1,0:T(8,128)(2,1)}, bf16[512,4096]{1,0:T(8,128)(2,1)S(1)}, u32[]{:S(2)}) copy-start(bf16[512,4096]{1,0:T(8,128)(2,1)S(1)} %get-tuple-element.14) | copy-start | bytes 12582916
  16.4 10.1 %copy-start.4 = (bf16[64,2,4096]{2,1,0:T(2,128)(2,1)S(1)}, bf16[64,2,4096]{2,1,0:T(2,128)(2,1)}, u32[]{:S(2)}) copy-start(bf16[64,2,4096]{2,1,0:T(2,128)(2,1)} %param.8) | copy-start | bytes 3145732
  23.3 3.2 %copy-start = (bf16[512,2,4096]{2,0,1:T(8,128)(2,1)}, bf16[512,2,4096]{2,0,1:T(8,128)(2,1)S(1)}, u32[]{:S(2)}) copy-start(bf16[512,2,4096]{2,0,1:T(8,128)(2,1)S(1)} %multiply_convert_fusion) | copy-start | bytes 25165828
  23.3 7.3 %copy-start.6 = (f32[512]{0:T(512)S(1)}, f32[512]{0:T(512)}, u32[]{:S(2)}) copy-start(f32[512]{0:T(512)} %param.9) | copy-start | bytes 6148
  30.6 4.3 %collective-permute-start.2 = (f32[512]{0:T(512)S(1)}, f32[512]{0:T(512)S(1)}, u32[]{:S(2)}, u32[]{:S(2)}) collective-permute-start(f32[512]{0:T(512)S(1)} %copy-done.6), channel_id=1, source_target_pairs={{0,30},{2,0},{4,2},{6,4},{8,6},{10,8},{12,10},{14,12},{16,14},{18,... | collective-permute-start | bytes 6152 | tf_op jit(solution)/shard_map/ppermute | solution.py:15
  31.9 3.6 %collective-permute-start.3 = (f32[512]{0:T(512)S(1)}, f32[512]{0:T(512)S(1)}, u32[]{:S(2)}, u32[]{:S(2)}) collective-permute-start(f32[512]{0:T(512)S(1)} %copy-done.6), channel_id=1, source_target_pairs={{0,28},{2,30},{4,0},{6,2},{8,4},{10,6},{12,8},{14,10},{16,12},{18,... | collective-permute-start | bytes 6152 | tf_op jit(solution)/shard_map/ppermute | solution.py:15
  34.9 8.2 %copy-start.1 = (bf16[512,2,4096]{2,0,1:T(8,128)(2,1)S(1)}, bf16[512,2,4096]{2,0,1:T(8,128)(2,1)}, u32[]{:S(2)}) copy-start(bf16[512,2,4096]{2,0,1:T(8,128)(2,1)} %copy-done) | copy-start | bytes 25165828
  35.8 10.3 %collective-permute-start.6 = (bf16[64,2,4096]{2,0,1:T(8,128)(2,1)S(1)}, bf16[64,2,4096]{2,0,1:T(8,128)(2,1)S(1)}, u32[]{:S(2)}, u32[]{:S(2)}) collective-permute-start(bf16[64,2,4096]{2,0,1:T(8,128)(2,1)S(1)} %collective-permute-done), channel_id=1, source_target_pairs={{0,2},{4,6},{8,10},{12,14},{16,18},{20,22},{24,26},{28,30},{1,3},{... | collective-permute-start | bytes 3145736 | tf_op jit(solution)/shard_map/ppermute | solution.py:21
  37.6 8.4 %collective-permute-start.4 = (f32[64,512]{1,0:T(8,128)S(1)}, f32[64,512]{1,0:T(8,128)S(1)}, u32[]{:S(2)}, u32[]{:S(2)}) collective-permute-start(f32[64,512]{1,0:T(8,128)S(1)} %convolution_subtract_fusion), channel_id=1, source_target_pairs={{0,1},{1,0},{2,3},{3,2},{4,5},{5,4},{6,7},{7,6},{8,9},{9,8},{10,11... | collective-permute-start | bytes 393224 | tf_op jit(solution)/shard_map/ppermute | solution.py:15
  43.1 3.1 %copy-start.3 = (bf16[512,4096]{1,0:T(8,128)(2,1)S(1)}, bf16[512,4096]{1,0:T(8,128)(2,1)}, u32[]{:S(2)}) copy-start(bf16[512,4096]{1,0:T(8,128)(2,1)} %copy-done.2) | copy-start | bytes 12582916
  45.8 6.4 %collective-permute-start.5 = (f32[64,512]{1,0:T(8,128)S(1)}, f32[64,512]{1,0:T(8,128)S(1)}, u32[]{:S(2)}, u32[]{:S(2)}) collective-permute-start(f32[64,512]{1,0:T(8,128)S(1)} %fusion.54), channel_id=1, source_target_pairs={{0,1},{1,0},{2,3},{3,2},{4,5},{5,4},{6,7},{7,6},{8,9},{9,8},{10,11... | collective-permute-start | bytes 393224 | tf_op jit(solution)/shard_map/ppermute | solution.py:15
  50.3 5.0 %collective-permute-start.7 = (f32[64,512]{1,0:T(8,128)S(1)}, f32[64,512]{1,0:T(8,128)S(1)}, u32[]{:S(2)}, u32[]{:S(2)}) collective-permute-start(f32[64,512]{1,0:T(8,128)S(1)} %fusion.53), channel_id=1, source_target_pairs={{0,1},{1,0},{2,3},{3,2},{4,5},{5,4},{6,7},{7,6},{8,9},{9,8},{10,11... | collective-permute-start | bytes 393224 | tf_op jit(solution)/shard_map/ppermute | solution.py:15
  55.5 13.9 %copy-start.5 = (f32[512]{0:T(512)}, f32[512]{0:T(512)S(1)}, u32[]{:S(2)}) copy-start(f32[512]{0:T(512)S(1)} %add_select_fusion) | copy-start | bytes 6148
  57.3 6.1 %collective-permute-start.12 = (bf16[64,512]{1,0:T(8,128)(2,1)S(1)}, bf16[64,512]{1,0:T(8,128)(2,1)S(1)}, u32[]{:S(2)}, u32[]{:S(2)}) collective-permute-start(bf16[64,512]{1,0:T(8,128)(2,1)S(1)} %get-tuple-element.41), channel_id=1, source_target_pairs={{0,30},{2,0},{4,2},{6,4},{8,6},{10,8},{12,10},{14,12},{16,14},{18,... | collective-permute-start | bytes 196616 | tf_op jit(solution)/shard_map/ppermute | solution.py:15
  59.5 10.4 %collective-permute-start.10 = (bf16[64,2,2048]{2,0,1:T(8,128)(2,1)S(1)}, bf16[64,2,2048]{2,0,1:T(8,128)(2,1)S(1)}, u32[]{:S(2)}, u32[]{:S(2)}) collective-permute-start(bf16[64,2,2048]{2,0,1:T(8,128)(2,1)S(1)} %fusion.50), channel_id=1, source_target_pairs={{0,30},{2,0},{4,2},{6,4},{8,6},{10,8},{12,10},{14,12},{16,14},{18,... | collective-permute-start | bytes 1572872 | tf_op jit(solution)/shard_map/ppermute | solution.py:15
  63.1 19.0 %collective-permute-start.13 = (bf16[64,512]{1,0:T(8,128)(2,1)S(1)}, bf16[64,512]{1,0:T(8,128)(2,1)S(1)}, u32[]{:S(2)}, u32[]{:S(2)}) collective-permute-start(bf16[64,512]{1,0:T(8,128)(2,1)S(1)} %get-tuple-element.40), channel_id=1, source_target_pairs={{0,28},{2,30},{4,0},{6,2},{8,4},{10,6},{12,8},{14,10},{16,12},{18,... | collective-permute-start | bytes 196616 | tf_op jit(solution)/shard_map/ppermute | solution.py:15
  63.1 13.2 %collective-permute-start.8 = (bf16[64,2,2048]{2,0,1:T(8,128)(2,1)S(1)}, bf16[64,2,2048]{2,0,1:T(8,128)(2,1)S(1)}, u32[]{:S(2)}, u32[]{:S(2)}) collective-permute-start(bf16[64,2,2048]{2,0,1:T(8,128)(2,1)S(1)} %fusion.47), channel_id=1, source_target_pairs={{0,30},{2,0},{4,2},{6,4},{8,6},{10,8},{12,10},{14,12},{16,14},{18,... | collective-permute-start | bytes 1572872 | tf_op jit(solution)/shard_map/ppermute | solution.py:15
  70.8 19.0 %collective-permute-start.11 = (bf16[64,2,2048]{2,0,1:T(8,128)(2,1)S(1)}, bf16[64,2,2048]{2,0,1:T(8,128)(2,1)S(1)}, u32[]{:S(2)}, u32[]{:S(2)}) collective-permute-start(bf16[64,2,2048]{2,0,1:T(8,128)(2,1)S(1)} %add_convert_fusion), channel_id=1, source_target_pairs={{0,30},{2,0},{4,2},{6,4},{8,6},{10,8},{12,10},{14,12},{16,14},{18,... | collective-permute-start | bytes 1572872 | tf_op jit(solution)/shard_map/ppermute | solution.py:15
  77.1 11.8 %collective-permute-start.9 = (bf16[64,2,2048]{2,0,1:T(8,128)(2,1)S(1)}, bf16[64,2,2048]{2,0,1:T(8,128)(2,1)S(1)}, u32[]{:S(2)}, u32[]{:S(2)}) collective-permute-start(bf16[64,2,2048]{2,0,1:T(8,128)(2,1)S(1)} %add_convert_fusion.1), channel_id=1, source_target_pairs={{0,30},{2,0},{4,2},{6,4},{8,6},{10,8},{12,10},{14,12},{16,14},{18,... | collective-permute-start | bytes 1572872 | tf_op jit(solution)/shard_map/ppermute | solution.py:15

commit v4 on v3

--- a/solution.py
+++ b/solution.py
@@ -26,7 +26,7 @@
     rest = shifted - jnp.round(shifted)
     y = 0.25 - jnp.abs(rest)
     square = y * y
-    coefficients = [TURN ** k / math.factorial(k) * (1 if k % 4 == 3 else -1) for k in (1, 3, 5, 7, 9, 11)]
+    coefficients = [-6.283185159611165, 41.341654929343306, -81.6009981926032, 76.54965682039136, -39.535813709565026]
     value = jnp.full_like(square, coefficients[-1])
     for coefficient in coefficients[-2::-1]:
         value = value * square + coefficient
@@ -64,12 +64,7 @@
         return crossed - quadratic
 
     mine = partial(references)
-    mine, defocus_sent = lax.optimization_barrier((mine, defocus))
-    defocus_1 = passed_along(defocus_sent, "blk", -1)
-    defocus_2 = passed_along(defocus_sent, "blk", -2)
-    mine, first, direct, defocus_1, defocus_2 = lax.optimization_barrier(
-        (mine, first, direct, defocus_1, defocus_2)
-    )
+    mine, first, direct = lax.optimization_barrier((mine, first, direct))
     paired = passed_by_even(first, "blk", 1)
     parts = [mine + passed_along(mine, "shell", 1)]
     even = lax.rem(lax.axis_index("blk"), 2) == 0
@@ -94,22 +89,32 @@
             "ri,ikp->rkp", rows, filtered[:, :, cut], preferred_element_type=jnp.float32
         )
 
-    returned_1 = passed_along(back_1, "blk", -1)
-    returned_2 = passed_along(back_2, "blk", -2)
+    high = lax.reduce_precision(defocus, 8, 7)
+    middle = lax.reduce_precision(defocus - high, 8, 7)
+    low = defocus - high - middle
+    rows = jnp.stack([high, middle, low] + [jnp.zeros_like(low)] * 13).astype(jnp.bfloat16)
+
+    def returned(values, steps):
+        got = passed_along(jnp.concatenate([values, rows], 0), "blk", -steps)
+        terms = got[per_block : per_block + 3].astype(jnp.float32)
+        return got[:per_block], terms[0] + terms[1] + terms[2]
+
+    returned_1, defocus_1 = returned(back_1, 1)
+    returned_2, defocus_2 = returned(back_2, 2)
     farther = [passed_along(sums(back_2, cut).astype(jnp.bfloat16), "blk", -1) for cut in columns]
     joined = [
         (sums(back_1, cut) + got.astype(jnp.float32)).astype(jnp.bfloat16)
         for cut, got in zip(columns, farther)
     ]
     nearer = [passed_along(value, "blk", -1) for value in joined]
-    defocus_2, _ = lax.optimization_barrier((defocus_2, joined[-1]))
+    defocus_2, here_later, _ = lax.optimization_barrier((defocus_2, here, joined[-1]))
     numerator = jnp.concatenate(
         [sums(here, cut) + got.astype(jnp.float32) for cut, got in zip(columns, nearer)], 2
     )
     denominator = sum(
-        jnp.einsum("ri,ip->rp", rows, values, preferred_element_type=jnp.float32)
-        for rows, values in (
-            (here, envelope),
+        jnp.einsum("ri,ip->rp", block, values, preferred_element_type=jnp.float32)
+        for block, values in (
+            (here_later, envelope),
             (returned_1, envelope_of(defocus_1)),
             (returned_2, envelope_of(defocus_2)),
         )

time: 94.1 us -> 102 us (1.084)
  starting transfers between devices: 29.4 us -> 19.6 us
  waiting for transfers between devices: 5.08 us -> 14 us
  matrix products: 33.1 us -> 40.9 us
    ppermute x12 -> x10, starting transfers between devices: 23.1 us -> 13.6 us  [passed_along(): return lax.ppermute(value, axis, pairs)]
    dot_general x6, matrix products: 5.06 us -> 11.6 us  [sums(): jnp.einsum('ri,ikp->rkp', rows, filtered[:, :, cut], preferred_element_ty...]
    ppermute x12 -> x10, waiting for transfers between devices: 5.07 us -> 11.1 us  [passed_along(): return lax.ppermute(value, axis, pairs)]
    another operation x0 -> x5, local copies, waits for them, and re-layouts: none -> 4.04 us  [body(): jnp.stack([high, middle, low] + [jnp.zeros_like(low)] * 13)]
    unnamed x19 -> x31, local copies, waits for them, and re-layouts: 6.19 us -> 3.01 us
    ppermute x2, waiting for transfers between devices: 0.01 us -> 2.84 us  [passed_by_even(): return lax.ppermute(value, axis, pairs)]
    dot_general x3, matrix products: 13.7 us -> 14.8 us  [body(): jnp.einsum('ri,ip->rp', block, values, preferred_element_type=jnp.float32)]
    unnamed x2 -> x3, other arithmetic: 2.1 us -> 2.1 us
  transfers between devices with their start and end apart: 14 -> 12, of which waited for: 4 -> 4; matrix products, arithmetic and copies ran while one was open for 49% -> 58% of each run, Pallas kernels for 0% -> 0%
where the time goes in v4:
time: 102 us
  matrix products  40.9 us (40%)
  starting transfers between devices  19.6 us (19%)
  other arithmetic  18.4 us (18%)
  waiting for transfers between devices  14 us (14%)
  local copies, waits for them, and re-layouts  7.15 us (7%)
  between operations  1.86 us (2%)
    dot_general x3, matrix products, body(): jnp.einsum('ri,ip->rp', block, values, preferred_element_type=jnp.float32)  14.8 us
    ppermute x10, starting transfers between devices, passed_along(): return lax.ppermute(value, axis, pairs)  13.6 us
    dot_general x6, matrix products, sums(): jnp.einsum('ri,ikp->rkp', rows, filtered[:, :, cut], preferred_element_ty...  11.6 us
    ppermute x10, waiting for transfers between devices, passed_along(): return lax.ppermute(value, axis, pairs)  11.1 us
    dot_general x3, matrix products, partial(): jnp.einsum('rkp,ikp->ri', block, filtered, preferred_element_type=jnp.flo...  8 us
    convert_element_type x1, other arithmetic, body(): (images.astype(jnp.float32) * (contrast * weight)[:, None, :]).astype(jnp...  6.89 us
    dot_general x3, matrix products, partial(): jnp.einsum('rp,ip->ri', power, envelope, preferred_element_type=jnp.float32)  6.42 us
    convert_element_type x1, other arithmetic, body(): envelope = (contrast * contrast * half_weight).astype(jnp.bfloat16)  6.36 us
  transfers between devices with their start and end apart: 12, of which 4 were waited for; matrix products, arithmetic and copies ran while one was open for 58% of the time, Pallas kernels for 0%

profile of v4, /device:TPU:0, one launch (start us, length us, event | category | flops | bytes accessed | tf_op | source)
XLA Modules:
  0.0 101.9 jit_solution(18257192053772784694)
XLA Ops:
  0.6 0.0 slice-start.2
  0.6 2.1 %fusion.114 = (bf16[64,2,4096]{2,0,1:T(8,128)(2,1)S(1)}, f32[64,2,4096]{2,0,1:T(8,128)S(1)}) fusion(bf16[64,2,4096]{2,1,0:T(2,128)(2,1)} %param.8), kind=kLoop, calls=%fused_computation.146 | loop fusion | flops 524288 | bytes 4194304 | tf_op args[1]
  2.7 0.5 collective-permute-start
  3.3 4.4 %collective-permute-start.1 = (bf16[64,2,4096]{2,0,1:T(8,128)(2,1)S(1)}, bf16[64,2,4096]{2,0,1:T(8,128)(2,1)S(1)}, u32[]{:S(2)}, u32[]{:S(2)}) collective-permute-start(bf16[64,2,4096]{2,0,1:T(8,128)(2,1)S(1)} %get-tuple-element.32), channel_id=1, source_target_pairs={{0,4},{4,8},{8,12},{12,16},{16,20},{20,24},{24,28},{28,0},{1,5},{5... | collective-permute-start | bytes 3145736 | tf_op jit(solution)/shard_map/ppermute | solution.py:21
  7.7 1.0 select_reduce_fusion
  8.7 0.7 broadcast_multiply_fusion.1
  9.4 0.0 slice-start.3
  9.4 6.4 %multiply_convert_fusion.3 = (bf16[512,4096]{1,0:T(8,128)(2,1)S(1)}, f32[512,4096]{1,0:T(8,128)S(1)}) fusion(f32[4096]{0:T(1024)S(1)} %get-tuple-element.39, f32[4096]{0:T(1024)S(1)} %get-tuple-element.44, f32[512]{0:T(512)} %param.9, f32[4096]{0:T(1024)S(1)} %get-tuple-element.40), kind=kLoop, calls=%fused_computation.20 | loop fusion | flops 41943040 | bytes 12634112 | tf_op jit(solution)/shard_map/convert_element_type | solution.py:52
  15.8 0.0 copy-start.3
  15.8 6.9 %multiply_convert_fusion = bf16[512,2,4096]{2,0,1:T(8,128)(2,1)S(1)} fusion(bf16[512,2,4096]{2,1,0:T(2,128)(2,1)S(1)} %bitcast.61, f32[512,4096]{1,0:T(8,128)S(1)} %get-tuple-element.38), kind=kLoop, calls=%fused_computation | loop fusion | flops 12582912 | bytes 25165824 | tf_op jit(solution)/shard_map/convert_element_type | solution.py:51
  22.7 0.0 copy-done.4
  22.8 0.0 copy-start
  22.8 0.0 copy-done.3
  22.8 2.7 %convolution_bitcast_fusion.2 = f32[64,512]{1,0:T(8,128)S(1)} fusion(bf16[512,2,4096]{2,0,1:T(8,128)(2,1)S(1)} %multiply_convert_fusion, bf16[64,2,4096]{2,1,0:T(2,128)(2,1)S(1)} %copy-done.3), kind=kOutput, calls=%fused_computation.67 | convolution fusion | flops 536870912 | bytes 9568256 | tf_op jit(solution)/shard_map/rkp,ikp->ri/dot_general | solution.py:62
  25.5 1.4 %convolution_subtract_fusion = f32[64,512]{1,0:T(8,128)S(1)} fusion(f32[64,512]{1,0:T(8,128)S(1)} %convolution_bitcast_fusion.2, bf16[512,4096]{1,0:T(8,128)(2,1)S(1)} %get-tuple-element.11, f32[64,2,4096]{2,0,1:T(8,128)S(1)} %get-tuple-element.33), kind=kOutput, calls=%fused_computation.62 | convolution fusion | flops 269516800 | bytes 6553600 | tf_op jit(solution)/shard_map/rp,ip->ri/dot_general | solution.py:63
  26.9 2.3 %collective-permute-done = bf16[64,2,4096]{2,0,1:T(8,128)(2,1)S(1)} collective-permute-done((bf16[64,2,4096]{2,0,1:T(8,128)(2,1)S(1)}, bf16[64,2,4096]{2,0,1:T(8,128)(2,1)S(1)}, u32[]{:S(2)}, u32[]{:S(2)}) %collective-permute-start) | collective-permute-done | bytes 1048608 | tf_op jit(solution)/shard_map/ppermute | solution.py:15
  29.1 2.8 %collective-permute-done.1 = bf16[64,2,4096]{2,0,1:T(8,128)(2,1)S(1)} collective-permute-done((bf16[64,2,4096]{2,0,1:T(8,128)(2,1)S(1)}, bf16[64,2,4096]{2,0,1:T(8,128)(2,1)S(1)}, u32[]{:S(2)}, u32[]{:S(2)}) %collective-permute-start.1) | collective-permute-done | bytes 1048608 | tf_op jit(solution)/shard_map/ppermute | solution.py:21
  32.0 0.2 convert_element_type.82
  32.2 1.5 %collective-permute-start.4 = (bf16[64,2,4096]{2,0,1:T(8,128)(2,1)S(1)}, bf16[64,2,4096]{2,0,1:T(8,128)(2,1)S(1)}, u32[]{:S(2)}, u32[]{:S(2)}) collective-permute-start(bf16[64,2,4096]{2,0,1:T(8,128)(2,1)S(1)} %collective-permute-done), channel_id=1, source_target_pairs={{0,2},{4,6},{8,10},{12,14},{16,18},{20,22},{24,26},{28,30},{1,3},{... | collective-permute-start | bytes 3145736 | tf_op jit(solution)/shard_map/ppermute | solution.py:21
  33.7 1.4 %fusion.59 = f32[64,512]{1,0:T(8,128)S(1)} fusion(bf16[512,4096]{1,0:T(8,128)(2,1)S(1)} %get-tuple-element.11, f32[64,2,4096]{2,0,1:T(8,128)S(1)} %convert_element_type.82), kind=kOutput, calls=%fused_computation.89 | convolution fusion | flops 269484032 | bytes 6422528 | tf_op jit(solution)/shard_map/rp,ip->ri/dot_general | solution.py:63
  35.2 2.7 %fusion.49 = f32[64,512]{1,0:T(8,128)S(1)} fusion(f32[64,512]{1,0:T(8,128)S(1)} %fusion.59, bf16[64,2,4096]{2,0,1:T(8,128)(2,1)S(1)} %collective-permute-done, bf16[512,2,4096]{2,0,1:T(8,128)(2,1)S(1)} %multiply_convert_fusion), kind=kOutput, calls=%fused_computation.66 | convolution fusion | flops 536903680 | bytes 9699328 | tf_op jit(solution)/shard_map/rkp,ikp->ri/dot_general | solution.py:62
  37.8 2.0 %collective-permute-start.3 = (f32[64,512]{1,0:T(8,128)S(1)}, f32[64,512]{1,0:T(8,128)S(1)}, u32[]{:S(2)}, u32[]{:S(2)}) collective-permute-start(f32[64,512]{1,0:T(8,128)S(1)} %fusion.49), channel_id=1, source_target_pairs={{0,1},{1,0},{2,3},{3,2},{4,5},{5,4},{6,7},{7,6},{8,9},{9,8},{10,11... | collective-permute-start | bytes 393224 | tf_op jit(solution)/shard_map/ppermute | solution.py:15
  39.8 0.6 fusion.89
  41.2 1.4 %stack.20 = bf16[1,512]{1,0:T(2,128)(2,1)} reshape(bf16[512]{0:T(512)(128)(2,1)} %get-tuple-element.43) | data formatting | bytes 2048 | tf_op jit(solution)/shard_map/stack | solution.py:95
  42.6 1.4 %stack.21 = bf16[1,512]{1,0:T(2,128)(2,1)} reshape(bf16[512]{0:T(512)(128)(2,1)} %get-tuple-element.42) | data formatting | bytes 2048 | tf_op jit(solution)/shard_map/stack | solution.py:95
  44.0 1.2 %stack.22 = bf16[1,512]{1,0:T(2,128)(2,1)} reshape(bf16[512]{0:T(512)(128)(2,1)} %get-tuple-element.41) | data formatting | bytes 2048 | tf_op jit(solution)/shard_map/stack | solution.py:95
  45.2 0.1 collective-permute-start.2
  45.3 0.0 collective-permute-done.3
  45.4 0.0 collective-permute-done.4
  45.4 0.1 fusion.64
  45.5 3.6 %fusion.62 = f32[64,512]{1,0:T(8,128)S(1)} fusion(bf16[512,4096]{1,0:T(8,128)(2,1)} %copy-done.2, f32[64,2,4096]{2,0,1:T(8,128)S(1)} %fusion.64), kind=kOutput, calls=%fused_computation.91 | convolution fusion | flops 269484032 | bytes 6422528 | tf_op jit(solution)/shard_map/rp,ip->ri/dot_general | solution.py:63
  49.1 0.0 copy-start.6
  49.2 2.7 %fusion.48 = f32[64,512]{1,0:T(8,128)S(1)} fusion(f32[64,512]{1,0:T(8,128)S(1)} %fusion.62, bf16[512,2,4096]{2,0,1:T(8,128)(2,1)S(1)} %copy-done.1, bf16[64,2,4096]{2,0,1:T(8,128)(2,1)S(1)} %collective-permute-done.1, bf16[64,2,4096]{2,0,1:T(8,128)(2,1)S(1)} %collective-permute-done.4, pred[]{:T(512)S(6)} %eq.19), kind=kOutput, calls=%fused_computation.64 | convolution fusion | flops 537427968 | bytes 10747905 | tf_op jit(solution)/shard_map/rkp,ikp->ri/dot_general | solution.py:62
  51.8 2.0 %collective-permute-start.5 = (f32[64,512]{1,0:T(8,128)S(1)}, f32[64,512]{1,0:T(8,128)S(1)}, u32[]{:S(2)}, u32[]{:S(2)}) collective-permute-start(f32[64,512]{1,0:T(8,128)S(1)} %fusion.48), channel_id=1, source_target_pairs={{0,1},{1,0},{2,3},{3,2},{4,5},{5,4},{6,7},{7,6},{8,9},{9,8},{10,11... | collective-permute-start | bytes 393224 | tf_op jit(solution)/shard_map/ppermute | solution.py:15
  53.9 0.0 collective-permute-done.2
  53.9 3.0 %collective-permute-done.5 = f32[64,512]{1,0:T(8,128)S(1)} collective-permute-done((f32[64,512]{1,0:T(8,128)S(1)}, f32[64,512]{1,0:T(8,128)S(1)}, u32[]{:S(2)}, u32[]{:S(2)}) %collective-permute-start.5) | collective-permute-done | bytes 131104 | tf_op jit(solution)/shard_map/ppermute | solution.py:15
  56.9 0.1 exponential_reduce_fusion
  57.0 0.1 select_convert_fusion
  57.1 0.8 fusion.45
  58.1 2.4 %collective-permute-start.10 = (bf16[80,512]{1,0:T(8,128)(2,1)S(1)}, bf16[80,512]{1,0:T(8,128)(2,1)S(1)}, u32[]{:S(2)}, u32[]{:S(2)}) collective-permute-start(bf16[80,512]{1,0:T(8,128)(2,1)S(1)} %concatenate.16), channel_id=1, source_target_pairs={{0,28},{2,30},{4,0},{6,2},{8,4},{10,6},{12,8},{14,10},{16,12},{18,... | collective-permute-start | bytes 245768 | tf_op jit(solution)/shard_map/ppermute | solution.py:15
  60.4 3.0 %fusion.42 = bf16[64,2,2048]{2,0,1:T(8,128)(2,1)S(1)} fusion(bf16[512,2,4096]{2,0,1:T(8,128)(2,1)} %copy-done, bf16[192,512]{1,0:T(8,128)(2,1)S(1)} %select_convert_fusion), kind=kOutput, calls=%fused_computation.59 | convolution fusion | flops 268697600 | bytes 4784128 | tf_op jit(solution)/shard_map/ri,ikp->rkp/dot_general | solution.py:88
  63.5 0.0 copy-start.5
  63.5 0.1 collective-permute-start.8
  63.6 1.6 %collective-permute-start.11 = (bf16[80,512]{1,0:T(8,128)(2,1)S(1)}, bf16[80,512]{1,0:T(8,128)(2,1)S(1)}, u32[]{:S(2)}, u32[]{:S(2)}) collective-permute-start(bf16[80,512]{1,0:T(8,128)(2,1)S(1)} %concatenate.17), channel_id=1, source_target_pairs={{0,30},{2,0},{4,2},{6,4},{8,6},{10,8},{12,10},{14,12},{16,14},{18,... | collective-permute-start | bytes 245768 | tf_op jit(solution)/shard_map/ppermute | solution.py:15
  65.1 0.1 collective-permute-start.6
  65.2 0.0 collective-permute-done.10
  65.2 5.9 %collective-permute-done.11 = bf16[80,512]{1,0:T(8,128)(2,1)S(1)} collective-permute-done((bf16[80,512]{1,0:T(8,128)(2,1)S(1)}, bf16[80,512]{1,0:T(8,128)(2,1)S(1)}, u32[]{:S(2)}, u32[]{:S(2)}) %collective-permute-start.11) | collective-permute-done | bytes 81952 | tf_op jit(solution)/shard_map/ppermute | solution.py:15
  71.1 0.0 collective-permute-done.8
  71.1 3.0 %add_convert_fusion = bf16[64,2,2048]{2,0,1:T(8,128)(2,1)S(1)} fusion(bf16[64,2,2048]{2,0,1:T(8,128)(2,1)S(1)} %collective-permute-done.8, bf16[512,2,4096]{2,0,1:T(8,128)(2,1)} %copy-done, bf16[192,512]{1,0:T(8,128)(2,1)S(1)} %select_convert_fusion), kind=kOutput, calls=%fused_computation.81 | convolution fusion | flops 269221888 | bytes 5308416 | tf_op jit(solution)/shard_map/ri,ikp->rkp/dot_general | solution.py:88
  74.2 4.7 %collective-permute-start.9 = (bf16[64,2,2048]{2,0,1:T(8,128)(2,1)S(1)}, bf16[64,2,2048]{2,0,1:T(8,128)(2,1)S(1)}, u32[]{:S(2)}, u32[]{:S(2)}) collective-permute-start(bf16[64,2,2048]{2,0,1:T(8,128)(2,1)S(1)} %add_convert_fusion), channel_id=1, source_target_pairs={{0,30},{2,0},{4,2},{6,4},{8,6},{10,8},{12,10},{14,12},{16,14},{18,... | collective-permute-start | bytes 1572872 | tf_op jit(solution)/shard_map/ppermute | solution.py:15
  78.8 3.1 %fusion.116 = f32[64,4096]{1,0:T(8,128)S(1)} fusion(bf16[64,512]{1,0:T(8,128)(2,1)S(1)} %get-tuple-element.15, bf16[512,4096]{1,0:T(8,128)(2,1)} %copy-done.2), kind=kOutput, calls=%fused_computation.148 | convolution fusion | flops 268435456 | bytes 5308416 | tf_op jit(solution)/shard_map/ri,ip->rp/dot_general | solution.py:115
  81.9 0.0 collective-permute-done.6
  81.9 3.0 %add_convert_fusion.1 = bf16[64,2,2048]{2,0,1:T(8,128)(2,1)S(1)} fusion(bf16[64,2,2048]{2,0,1:T(8,128)(2,1)S(1)} %collective-permute-done.6, bf16[512,2,4096]{2,0,1:T(8,128)(2,1)} %copy-done, bf16[192,512]{1,0:T(8,128)(2,1)S(1)} %select_convert_fusion), kind=kOutput, calls=%fused_computation.83 | convolution fusion | flops 269221888 | bytes 5308416 | tf_op jit(solution)/shard_map/ri,ikp->rkp/dot_general | solution.py:88
  85.0 0.3 collective-permute-start.7
  85.3 0.0 slice-start
  85.3 5.4 %convolution_add_fusion.1 = f32[64,4096]{1,0:T(8,128)S(1)} fusion(f32[64,4096]{1,0:T(8,128)S(1)} %fusion.116, f32[512]{0:T(512)S(1)} %bitcast.63, f32[4096]{0:T(1024)S(1)} %get-tuple-element.39, f32[4096]{0:T(1024)S(1)} %copy-done.5, bf16[80,512]{1,0:T(8,128)(2,1)S(1)} %collective-permute-done.11), kind=kOutput, calls=%fused_computation.27 | convolution fusion | flops 308543488 | bytes 2197504 | tf_op jit(solution)/shard_map/ri,ip->rp/dot_general | solution.py:115
  90.7 0.0 slice-start.1
  90.7 6.4 %convolution_add_fusion = f32[64,4096]{1,0:T(8,128)} fusion(f32[64,4096]{1,0:T(8,128)S(1)} %convolution_add_fusion.1, f32[512]{0:T(512)S(1)} %bitcast.62, f32[4096]{0:T(1024)S(1)} %get-tuple-element.39, f32[4096]{0:T(1024)S(1)} %copy-done.5, bf16[80,512]{1,0:T(8,128)(2,1)S(1)} %collective-permute-done.10), kind=kOutput, calls=%fused_computation.26 | convolution fusion | flops 308543488 | bytes 2197504 | tf_op jit(solution)/shard_map/ri,ip->rp/dot_general | solution.py:115
  97.1 0.0 collective-permute-done.7
  97.1 0.8 convert_add_fusion.1
  97.9 0.0 collective-permute-done.9
  97.9 0.8 convert_add_fusion
  98.8 0.1 pad_maximum_fusion
  98.9 2.9 %copy.26 = f32[64,2,4096]{2,1,0:T(2,128)} copy(f32[64,2,4096]{2,0,1:T(8,128)S(1)} %pad_maximum_fusion) | data formatting | bytes 4194304
  (38 shorter events, 0.3 us)
Async XLA Ops:
  0.6 15.2 %slice-start.2 = ((s8[8388608]{0:T(1024)(128)(4,1)}), s8[4194304]{0:T(1024)(128)(4,1)S(1)}, s32[]{:S(2)}) async-start(s8[8388608]{0:T(1024)(128)(4,1)} %bitcast.60), calls=%async_computation.2 | async-start | bytes 8388608
  2.7 26.4 %collective-permute-start = (bf16[64,2,4096]{2,0,1:T(8,128)(2,1)S(1)}, bf16[64,2,4096]{2,0,1:T(8,128)(2,1)S(1)}, u32[]{:S(2)}, u32[]{:S(2)}) collective-permute-start(bf16[64,2,4096]{2,0,1:T(8,128)(2,1)S(1)} %get-tuple-element.32), channel_id=1, source_target_pairs={{0,2},{2,4},{4,6},{6,8},{8,10},{10,12},{12,14},{14,16},{16,18},{18... | collective-permute-start | bytes 3145736 | tf_op jit(solution)/shard_map/ppermute | solution.py:15
  3.3 28.7 %collective-permute-start.1 = (bf16[64,2,4096]{2,0,1:T(8,128)(2,1)S(1)}, bf16[64,2,4096]{2,0,1:T(8,128)(2,1)S(1)}, u32[]{:S(2)}, u32[]{:S(2)}) collective-permute-start(bf16[64,2,4096]{2,0,1:T(8,128)(2,1)S(1)} %get-tuple-element.32), channel_id=1, source_target_pairs={{0,4},{4,8},{8,12},{12,16},{16,20},{20,24},{24,28},{28,0},{1,5},{5... | collective-permute-start | bytes 3145736 | tf_op jit(solution)/shard_map/ppermute | solution.py:21
  9.4 13.3 %copy-start.4 = (f32[4096]{0:T(1024)}, f32[4096]{0:T(1024)S(1)}, u32[]{:S(2)}) copy-start(f32[4096]{0:T(1024)S(1)} %get-tuple-element.44) | copy-start | bytes 49156
  9.4 6.4 %slice-start.3 = ((s8[8388608]{0:T(1024)(128)(4,1)}), s8[4194304]{0:T(1024)(128)(4,1)S(1)}, s32[]{:S(2)}) async-start(s8[8388608]{0:T(1024)(128)(4,1)} %bitcast.60), calls=%async_computation.3 | async-start | bytes 8388608
  15.8 17.9 %copy-start.2 = (bf16[512,4096]{1,0:T(8,128)(2,1)}, bf16[512,4096]{1,0:T(8,128)(2,1)S(1)}, u32[]{:S(2)}) copy-start(bf16[512,4096]{1,0:T(8,128)(2,1)S(1)} %get-tuple-element.11) | copy-start | bytes 12582916
  15.8 6.9 %copy-start.3 = (bf16[64,2,4096]{2,1,0:T(2,128)(2,1)S(1)}, bf16[64,2,4096]{2,1,0:T(2,128)(2,1)}, u32[]{:S(2)}) copy-start(bf16[64,2,4096]{2,1,0:T(2,128)(2,1)} %param.8) | copy-start | bytes 3145732
  22.8 12.4 %copy-start = (bf16[512,2,4096]{2,0,1:T(8,128)(2,1)}, bf16[512,2,4096]{2,0,1:T(8,128)(2,1)S(1)}, u32[]{:S(2)}) copy-start(bf16[512,2,4096]{2,0,1:T(8,128)(2,1)S(1)} %multiply_convert_fusion) | copy-start | bytes 25165828
  26.9 12.9 %copy-start.10 = (f32[512]{0:T(512)S(1)}, f32[512]{0:T(512)}, u32[]{:S(2)}) copy-start(f32[512]{0:T(512)} %param.9) | copy-start | bytes 6148
  32.2 13.2 %collective-permute-start.4 = (bf16[64,2,4096]{2,0,1:T(8,128)(2,1)S(1)}, bf16[64,2,4096]{2,0,1:T(8,128)(2,1)S(1)}, u32[]{:S(2)}, u32[]{:S(2)}) collective-permute-start(bf16[64,2,4096]{2,0,1:T(8,128)(2,1)S(1)} %collective-permute-done), channel_id=1, source_target_pairs={{0,2},{4,6},{8,10},{12,14},{16,18},{20,22},{24,26},{28,30},{1,3},{... | collective-permute-start | bytes 3145736 | tf_op jit(solution)/shard_map/ppermute | solution.py:21
  37.8 7.5 %collective-permute-start.3 = (f32[64,512]{1,0:T(8,128)S(1)}, f32[64,512]{1,0:T(8,128)S(1)}, u32[]{:S(2)}, u32[]{:S(2)}) collective-permute-start(f32[64,512]{1,0:T(8,128)S(1)} %fusion.49), channel_id=1, source_target_pairs={{0,1},{1,0},{2,3},{3,2},{4,5},{5,4},{6,7},{7,6},{8,9},{9,8},{10,11... | collective-permute-start | bytes 393224 | tf_op jit(solution)/shard_map/ppermute | solution.py:15
  40.4 8.7 %copy-start.1 = (bf16[512,2,4096]{2,0,1:T(8,128)(2,1)S(1)}, bf16[512,2,4096]{2,0,1:T(8,128)(2,1)}, u32[]{:S(2)}) copy-start(bf16[512,2,4096]{2,0,1:T(8,128)(2,1)} %copy-done) | copy-start | bytes 25165828
  45.2 8.6 %collective-permute-start.2 = (f32[64,512]{1,0:T(8,128)S(1)}, f32[64,512]{1,0:T(8,128)S(1)}, u32[]{:S(2)}, u32[]{:S(2)}) collective-permute-start(f32[64,512]{1,0:T(8,128)S(1)} %convolution_subtract_fusion), channel_id=1, source_target_pairs={{0,1},{1,0},{2,3},{3,2},{4,5},{5,4},{6,7},{7,6},{8,9},{9,8},{10,11... | collective-permute-start | bytes 393224 | tf_op jit(solution)/shard_map/ppermute | solution.py:15
  49.1 8.9 %copy-start.6 = (bf16[1,512]{1,0:T(2,128)(2,1)S(1)}, bf16[1,512]{1,0:T(2,128)(2,1)}, u32[]{:S(2)}) copy-start(bf16[1,512]{1,0:T(2,128)(2,1)} %stack.20) | copy-start | bytes 3076
  49.2 8.9 %copy-start.7 = (bf16[1,512]{1,0:T(2,128)(2,1)S(1)}, bf16[1,512]{1,0:T(2,128)(2,1)}, u32[]{:S(2)}) copy-start(bf16[1,512]{1,0:T(2,128)(2,1)} %stack.21) | copy-start | bytes 3076
  49.2 8.9 %copy-start.8 = (bf16[1,512]{1,0:T(2,128)(2,1)S(1)}, bf16[1,512]{1,0:T(2,128)(2,1)}, u32[]{:S(2)}) copy-start(bf16[1,512]{1,0:T(2,128)(2,1)} %stack.22) | copy-start | bytes 3076
  51.8 5.0 %collective-permute-start.5 = (f32[64,512]{1,0:T(8,128)S(1)}, f32[64,512]{1,0:T(8,128)S(1)}, u32[]{:S(2)}, u32[]{:S(2)}) collective-permute-start(f32[64,512]{1,0:T(8,128)S(1)} %fusion.48), channel_id=1, source_target_pairs={{0,1},{1,0},{2,3},{3,2},{4,5},{5,4},{6,7},{7,6},{8,9},{9,8},{10,11... | collective-permute-start | bytes 393224 | tf_op jit(solution)/shard_map/ppermute | solution.py:15
  57.0 24.9 %copy-start.9 = (f32[512]{0:T(512)}, f32[512]{0:T(512)S(1)}, u32[]{:S(2)}) copy-start(f32[512]{0:T(512)S(1)} %add_select_fusion) | copy-start | bytes 6148
  58.1 7.1 %collective-permute-start.10 = (bf16[80,512]{1,0:T(8,128)(2,1)S(1)}, bf16[80,512]{1,0:T(8,128)(2,1)S(1)}, u32[]{:S(2)}, u32[]{:S(2)}) collective-permute-start(bf16[80,512]{1,0:T(8,128)(2,1)S(1)} %concatenate.16), channel_id=1, source_target_pairs={{0,28},{2,30},{4,0},{6,2},{8,4},{10,6},{12,8},{14,10},{16,12},{18,... | collective-permute-start | bytes 245768 | tf_op jit(solution)/shard_map/ppermute | solution.py:15
  63.5 21.8 %copy-start.5 = (f32[4096]{0:T(1024)S(1)}, f32[4096]{0:T(1024)}, u32[]{:S(2)}) copy-start(f32[4096]{0:T(1024)} %copy-done.4) | copy-start | bytes 49156
  63.5 7.7 %collective-permute-start.8 = (bf16[64,2,2048]{2,0,1:T(8,128)(2,1)S(1)}, bf16[64,2,2048]{2,0,1:T(8,128)(2,1)S(1)}, u32[]{:S(2)}, u32[]{:S(2)}) collective-permute-start(bf16[64,2,2048]{2,0,1:T(8,128)(2,1)S(1)} %fusion.45), channel_id=1, source_target_pairs={{0,30},{2,0},{4,2},{6,4},{8,6},{10,8},{12,10},{14,12},{16,14},{18,... | collective-permute-start | bytes 1572872 | tf_op jit(solution)/shard_map/ppermute | solution.py:15
  63.6 7.5 %collective-permute-start.11 = (bf16[80,512]{1,0:T(8,128)(2,1)S(1)}, bf16[80,512]{1,0:T(8,128)(2,1)S(1)}, u32[]{:S(2)}, u32[]{:S(2)}) collective-permute-start(bf16[80,512]{1,0:T(8,128)(2,1)S(1)} %concatenate.17), channel_id=1, source_target_pairs={{0,30},{2,0},{4,2},{6,4},{8,6},{10,8},{12,10},{14,12},{16,14},{18,... | collective-permute-start | bytes 245768 | tf_op jit(solution)/shard_map/ppermute | solution.py:15
  65.1 16.8 %collective-permute-start.6 = (bf16[64,2,2048]{2,0,1:T(8,128)(2,1)S(1)}, bf16[64,2,2048]{2,0,1:T(8,128)(2,1)S(1)}, u32[]{:S(2)}, u32[]{:S(2)}) collective-permute-start(bf16[64,2,2048]{2,0,1:T(8,128)(2,1)S(1)} %fusion.42), channel_id=1, source_target_pairs={{0,30},{2,0},{4,2},{6,4},{8,6},{10,8},{12,10},{14,12},{16,14},{18,... | collective-permute-start | bytes 1572872 | tf_op jit(solution)/shard_map/ppermute | solution.py:15
  74.2 23.7 %collective-permute-start.9 = (bf16[64,2,2048]{2,0,1:T(8,128)(2,1)S(1)}, bf16[64,2,2048]{2,0,1:T(8,128)(2,1)S(1)}, u32[]{:S(2)}, u32[]{:S(2)}) collective-permute-start(bf16[64,2,2048]{2,0,1:T(8,128)(2,1)S(1)} %add_convert_fusion), channel_id=1, source_target_pairs={{0,30},{2,0},{4,2},{6,4},{8,6},{10,8},{12,10},{14,12},{16,14},{18,... | collective-permute-start | bytes 1572872 | tf_op jit(solution)/shard_map/ppermute | solution.py:15
  85.0 12.1 %collective-permute-start.7 = (bf16[64,2,2048]{2,0,1:T(8,128)(2,1)S(1)}, bf16[64,2,2048]{2,0,1:T(8,128)(2,1)S(1)}, u32[]{:S(2)}, u32[]{:S(2)}) collective-permute-start(bf16[64,2,2048]{2,0,1:T(8,128)(2,1)S(1)} %add_convert_fusion.1), channel_id=1, source_target_pairs={{0,30},{2,0},{4,2},{6,4},{8,6},{10,8},{12,10},{14,12},{16,14},{18,... | collective-permute-start | bytes 1572872 | tf_op jit(solution)/shard_map/ppermute | solution.py:15
  85.3 11.8 %slice-start = ((s8[8388608]{0:T(1024)(128)(4,1)}), s8[4194304]{0:T(1024)(128)(4,1)S(1)}, s32[]{:S(2)}) async-start(s8[8388608]{0:T(1024)(128)(4,1)} %bitcast.58), calls=%async_computation | async-start | bytes 8388608
  90.7 6.4 %slice-start.1 = ((s8[8388608]{0:T(1024)(128)(4,1)}), s8[4194304]{0:T(1024)(128)(4,1)S(1)}, s32[]{:S(2)}) async-start(s8[8388608]{0:T(1024)(128)(4,1)} %bitcast.58), calls=%async_computation.1 | async-start | bytes 8388608
